TPU v7x, 256 devices: a whole 4x4x8 slice. The times are simulated.
256 devices in a mesh: row: 32 (over z, y_hi, core), col: 8 (over x, y_lo).
Axes of the slice: x: 4, y: 4 (y_hi: 2, y_lo: 2; y = y_hi * 2 + y_lo), z: 8, core: 2. Of those that a mesh axis runs over, the one named last changes fastest.
Arguments:
- seq: float32 [1536, 1024], P('row', 'col'), may hold values from -6 to 6
- query: float32 [1536, 1024], P('row', 'col'), may hold values from -24 to 24, as said below
- key: float32 [1536, 1024], P('col', 'row'), may hold values from -24 to 24, as said below
- value: float32 [1536, 1024], P('col', 'row'), may hold values from -6 to 6
- pair: float32 [1536, 1536, 128], P('row', 'col'), may hold values from -6 to 6
- w_bias: float32 [128, 32], replicated, may hold values from -0.5 to 0.5
- w_out: float32 [1024, 1024], P(None, 'col'), may hold values from -0.75 to 0.75
- w_left: float32 [1024, 64], P('col'), may hold values from -0.1875 to 0.1875
- w_right: float32 [1024, 64], P('col'), may hold values from -0.1875 to 0.1875
- w_outer: float32 [128, 128], replicated, may hold values from -0.5 to 0.5
- outer_bias: float32 [128], replicated, may hold values from -3 to 3
- w_up: float32 [128, 512], replicated, may hold values from -0.5 to 0.5
- w_down: float32 [512, 128], replicated, may hold values from -0.25 to 0.25
Outputs:
- seq_new: float32 [1536, 1024], P('row', 'col')
- pair_new: float32 [1536, 1536, 128], P('row', 'col')
Inputs may be any that keep to these rules, and one draw needn't show every extreme that they name: `query`: Head-major queries of order one; some residues may be much larger. `key`: Head-major keys of order one; some residues may be much larger.
All inputs are finite; a program needn't handle non-finite values.
Results may differ from a plain program's by a relative error of at most 0.0003.
Values sent between devices are 32-bit elements; how exact they have to be, the bound alone decides.
No kernel may reach another device: no remote copies, remote signals or barrier semaphores. Data moves between devices by JAX's collectives and lax.ppermute only.
A program may use at most 64 MiB of HBM per device.

v0:
```python
import jax
import jax.numpy as jnp
from jax import lax
from jax.sharding import PartitionSpec as P

HIGH = lax.Precision.HIGHEST


def merged(x, axis, combine):
    everything = jax.tree.map(lambda part: lax.all_gather(part, axis), x)
    leading = jax.tree.map(lambda part: part[0], everything)

    def hop(k, so_far):
        return combine(so_far, jax.tree.map(lambda part: part[k], everything))

    return lax.fori_loop(1, lax.axis_size(axis), hop, leading)


def channel_norm(x):
    centre = x - jnp.mean(x, axis=-1, keepdims=True)
    return centre * lax.rsqrt(jnp.mean(centre * centre, axis=-1, keepdims=True) + 1e-05)


def combine(first, second):
    top = jnp.maximum(first[0], second[0])
    scale_one = jnp.exp(first[0] - top)
    scale_two = jnp.exp(second[0] - top)
    totals = first[1] * scale_one + second[1] * scale_two
    weighted = first[2] * scale_one[..., None] + second[2] * scale_two[..., None]
    return (top, totals, weighted)


def partial_softmax(q_heads, k_heads, v_heads, bias, scale):
    scores = jnp.einsum("ihd,jhd->ihj", q_heads, k_heads, precision=HIGH) * scale + bias
    top = jnp.max(scores, axis=2)
    expo = jnp.exp(scores - top[..., None])
    totals = jnp.sum(expo, axis=2)
    weighted = jnp.einsum("ihj,jhd->ihd", expo, v_heads, precision=HIGH)
    return (top, totals, weighted)


def per_device(
    seq, query, key, value, pair, w_bias, w_out, w_left, w_right, w_outer, outer_bias, w_up, w_down
):
    rows_here = pair.shape[0]
    cols_here = pair.shape[1]
    channels = pair.shape[2]
    heads = w_bias.shape[1]
    width = w_out.shape[0]
    head_dim = width // heads
    proj_width = w_left.shape[1]
    scale = 1.0 / jnp.sqrt(jnp.float32(head_dim))
    bias = jnp.einsum("ijc,ch->ihj", channel_norm(pair), w_bias, precision=HIGH)
    queries = lax.all_gather(query, "col", axis=1, tiled=True)
    keys_all, values_all = (
        lax.all_gather(key, "row", axis=1, tiled=True),
        lax.all_gather(value, "row", axis=1, tiled=True),
    )
    parts = partial_softmax(
        queries.reshape(rows_here, heads, head_dim),
        keys_all.reshape(cols_here, heads, head_dim),
        values_all.reshape(cols_here, heads, head_dim),
        bias,
        scale,
    )
    top, totals, weighted = merged(parts, "col", combine)
    attn = (weighted / totals[..., None]).reshape(rows_here, width)
    seq_new = seq + jnp.dot(attn, w_out, precision=HIGH)
    sum_value, sum_square = lax.psum(
        (jnp.sum(seq_new, axis=1), jnp.sum(seq_new * seq_new, axis=1)), "col"
    )
    mean_value = (sum_value / width)[:, None]
    mean_square = (sum_square / width)[:, None]
    seq_norm = (seq_new - mean_value) * lax.rsqrt(mean_square - mean_value * mean_value + 1e-05)
    left_part = jnp.dot(seq_norm, w_left, precision=HIGH)
    right_part = jnp.dot(seq_norm, w_right, precision=HIGH)
    left, right = lax.psum((left_part, right_part), "col")
    right_every = lax.all_gather(right, "row", axis=0, tiled=True)
    start = lax.axis_index("col") * cols_here
    right_block = lax.dynamic_slice_in_dim(right_every, start, cols_here, 0)
    w_prod = w_outer[:proj_width]
    w_diff = w_outer[proj_width:]
    table = right_block[:, :, None] * w_prod[None, :, :]
    left_diff = jnp.dot(left, w_diff, precision=HIGH)
    right_diff = jnp.dot(right_block, w_diff, precision=HIGH)
    outer = (
        jnp.einsum("ip,jpc->ijc", left, table, precision=HIGH)
        + left_diff[:, None, :]
        - right_diff[None, :, :]
        + outer_bias
    )
    pair_mid = pair + outer
    flat = pair_mid.reshape(rows_here * cols_here, channels)
    hidden_act = jax.nn.relu(jnp.dot(channel_norm(flat), w_up, precision=HIGH))
    pair_new = flat + jnp.dot(hidden_act, w_down, precision=HIGH)
    return (seq_new, pair_new.reshape(rows_here, cols_here, channels))


def solution(mesh):
    in_specs = (
        P("row", "col"),
        P("row", "col"),
        P("col", "row"),
        P("col", "row"),
        P("row", "col", None),
        P(),
        P(None, "col"),
        P("col", None),
        P("col", None),
        P(),
        P(),
        P(),
        P(),
    )
    out_specs = (P("row", "col"), P("row", "col", None))
    return jax.shard_map(
        per_device, mesh=mesh, in_specs=in_specs, out_specs=out_specs, check_vma=False
    )
```

profile of v0, /device:TPU:1, one launch (start us, length us, event | category | flops | bytes accessed | tf_op | source)
XLA Modules:
  0.0 464.2 jit_solution(14313563270270739162)
XLA Ops:
  7.3 4.1 reduce_sum.63
  11.4 4.9 %multiply_reduce_fusion.1 = f32[48,192]{1,0:T(8,128)S(1)} fusion(f32[48,192,128]{2,1,0:T(8,128)} %param.19, f32[48,192]{1,0:T(8,128)S(1)} %broadcast_multiply_fusion.1), kind=kLoop, calls=%fused_computation.22 | loop fusion | flops 3529728 | bytes 4792320 | tf_op jit(solution)/shard_map/reduce_sum | solution.py:21
  16.3 23.2 %all_gather.31 = f32[48,1024]{1,0:T(8,128)S(1)} all-gather(f32[48,128]{1,0:T(8,128)S(1)} %copy-done.8), channel_id=1, replica_groups=mesh['row'=32,'col'=8] {'col'}, dimensions={1}, use_global_device_ids=true | all-gather | bytes 221184 | tf_op jit(solution)/shard_map/all_gather | solution.py:54
  39.6 0.2 copy.44
  39.8 54.6 %all_gather.30 = f32[192,1024]{0,1:T(8,128)S(1)} all-gather(f32[192,32]{0,1:T(8,128)S(1)} %copy-done.4), channel_id=1, replica_groups=mesh['row'=32,'col'=8] {'row'}, dimensions={1}, use_global_device_ids=true | all-gather | bytes 811008 | tf_op jit(solution)/shard_map/all_gather | solution.py:56
  94.4 39.6 %all_gather.36 = f32[192,1024]{0,1:T(8,128)S(1)} all-gather(f32[192,32]{0,1:T(8,128)S(1)} %copy-done.5), channel_id=1, replica_groups=mesh['row'=32,'col'=8] {'row'}, dimensions={1}, use_global_device_ids=true | all-gather | bytes 811008 | tf_op jit(solution)/shard_map/all_gather | solution.py:57
  134.0 12.2 %fusion.12 = f32[48,192,32]{1,2,0:T(8,128)S(1)} fusion(f32[48,192,128]{2,1,0:T(8,128)} %param.19, f32[48,192]{1,0:T(8,128)S(1)} %add_rsqrt_fusion.1, f32[48,192]{1,0:T(8,128)S(1)} %broadcast_multiply_fusion.1, f32[128,32]{0,1:T(8,128)S(1)} %copy-done.9), kind=kOutput, calls=%fused_computation.20 | convolution fusion | flops 455344128 | bytes 5988352 | tf_op jit(solution)/shard_map/ijc,ch->ihj/dot_general | solution.py:53
  146.2 2.5 fusion.40
  148.7 1.8 fusion.23
  150.5 1.5 copy.46
  152.0 30.6 %all-gather.3 = f32[8,48,32]{1,2,0:T(8,128)S(1)} all-gather(f32[1,48,32]{1,2,0:T(8,128)S(1)} %bitcast.70), channel_id=2, replica_groups=mesh['row'=32,'col'=8] {'col'}, dimensions={0}, use_global_device_ids=true | all-gather | bytes 55296 | tf_op jit(solution)/shard_map/all_gather | solution.py:10
  182.7 0.1 copy.47
  182.8 0.5 fusion.22
  183.3 28.0 %all-gather.4 = f32[8,48,32]{1,2,0:T(8,128)S(1)} all-gather(f32[1,48,32]{1,2,0:T(8,128)S(1)} %bitcast.71), channel_id=3, replica_groups=mesh['row'=32,'col'=8] {'col'}, dimensions={0}, use_global_device_ids=true | all-gather | bytes 55296 | tf_op jit(solution)/shard_map/all_gather | solution.py:10
  211.3 0.1 copy.48
  211.4 72.8 %all-gather.7.cloned.1.call-done = f32[384,32,32]{2,1,0:T(8,128)} async-done(((f32[48,32,32]{2,1,0:T(8,128)}), f32[384,32,32]{2,1,0:T(8,128)}) %all-gather.7.cloned.1.call-update) | async-done | bytes 1572880 | tf_op jit(solution)/shard_map/all_gather | solution.py:10
  284.1 1.2 slice.27
  285.4 13.6 %while.19 = (s32[]{:T(128)}, f32[48,32]{1,0:T(8,128)S(1)}, f32[48,32]{1,0:T(8,128)S(1)}, f32[48,32,32]{2,1,0:T(8,128)S(1)}, f32[8,48,32]{1,2,0:T(8,128)S(1)}, /*...) while((s32[]{:T(128)}, f32[48,32]{1,0:T(8,128)S(1)}, ...), condition=%wide.region_5.0_spmd, body=%wide.region_4.0_spmd.sunk | while | flops 156677 | bytes 700559 | solution.py:16
  285.4 0.1 copy.62
  285.6 1.7 fusion.58
  287.4 0.1 copy.62
  287.5 1.7 fusion.58
  289.3 0.1 copy.62
  289.5 1.7 fusion.58
  291.4 1.7 fusion.58
  293.4 1.7 fusion.58
  295.1 0.1 copy.62
  295.3 1.7 fusion.58
  297.3 1.7 fusion.58
  299.0 0.3 broadcast_divide_fusion
  299.3 0.4 reshape.84
  299.7 0.5 fusion.38
  300.2 16.0 %all-reduce.1 = (f32[48]{0:T(128)S(1)}, f32[48]{0:T(128)S(1)}) all-reduce(f32[48]{0:T(128)S(1)} %get-tuple-element.210, f32[48]{0:T(128)S(1)} %get-tuple-element.209), channel_id=1, replica_groups=mesh['row'=32,'col'=8] {'col'}, use_global_device_ids=true, to_apply=%region_9.0 | all-reduce | flops 96 | bytes 768 | tf_op jit(solution)/shard_map/psum | solution.py:69
  316.2 0.2 fusion.30
  316.5 0.2 fusion.31
  316.7 25.8 %all-reduce = (f32[48,64]{1,0:T(8,128)S(1)}, f32[48,64]{1,0:T(8,128)S(1)}) all-reduce(f32[48,64]{1,0:T(8,128)S(1)} %fusion.30, f32[48,64]{1,0:T(8,128)S(1)} %fusion.31), channel_id=1, replica_groups=mesh['row'=32,'col'=8] {'col'}, use_global_device_ids=true, to_apply=%region_11.0 | all-reduce | flops 6144 | bytes 49152 | tf_op jit(solution)/shard_map/psum | solution.py:77
  342.5 0.2 fusion.27
  342.6 52.4 %all_gather.39 = f32[1536,64]{1,0:T(8,128)S(1)} all-gather(f32[48,64]{1,0:T(8,128)S(1)} %get-tuple-element.225), channel_id=1, replica_groups=mesh['row'=32,'col'=8] {'row'}, dimensions={0}, use_global_device_ids=true | all-gather | bytes 405504 | tf_op jit(solution)/shard_map/all_gather | solution.py:78
  395.1 0.2 fusion.25
  395.3 12.3 %fusion.41 = (f32[48,192]{0,1:T(8,128)S(1)}, f32[48,192,128]{2,0,1:T(8,128)}) fusion(f32[128]{0:T(128)S(1)} %copy-done.10, f32[192,128]{1,0:T(8,128)S(1)} %fusion.25, f32[48,128]{1,0:T(8,128)S(1)} %fusion.27, f32[64,128]{1,0:T(8,128)S(1)} %slice-done.4, f32[192,64]{1,0:T(8,128)S(1)} %constant_dynamic-slice_fusion.2, f32[48,64]{1,0:T(8,128)S(1)} %get-tuple-element.226, ...), kind=kOutput, calls=%fused_computation.62 | convolution fusion | flops 913431552 | bytes 9691648 | tf_op jit(solution)/shard_map/ip,jpc->ijc/dot_general | solution.py:87
  407.7 0.1 div.35
  407.8 0.1 copy.54
  407.9 6.1 %copy.52 = f32[48,192,128]{2,1,0:T(8,128)} copy(f32[48,192,128]{2,0,1:T(8,128)} %get-tuple-element.241) | data formatting | bytes 9437184 | tf_op jit(solution)/shard_map/add | solution.py:92
  414.0 2.7 multiply_reduce_fusion
  416.9 0.1 rsqrt.26
  417.0 7.1 %fusion.11 = f32[9216,128]{1,0:T(8,128)S(1)} fusion(f32[48,192,128]{2,1,0:T(8,128)} %copy.52, f32[9216]{0:T(1024)S(1)} %rsqrt.26, f32[9216]{0:T(1024)S(1)} %div.35), kind=kLoop, calls=%fused_computation.17 | loop fusion | flops 2359296 | bytes 9510912 | tf_op jit(solution)/shard_map/mul | solution.py:21
  424.2 16.2 %fusion.42 = f32[9216,512]{1,0:T(8,128)S(1)} fusion(f32[9216,128]{1,0:T(8,128)S(1)} %fusion.11, f32[128,512]{1,0:T(8,128)S(1)} %copy-done.1), kind=kOutput, calls=%fused_computation.63 | convolution fusion | flops 7247757312 | bytes 23855104 | tf_op jit(solution)/shard_map/dot_general | solution.py:94
  440.4 16.7 %fusion.5 = f32[9216,128]{1,0:T(8,128)} fusion(f32[9216,128]{1,0:T(8,128)S(1)} %bitcast.62, f32[512,128]{1,0:T(8,128)S(1)} %copy-done.2, f32[9216,512]{1,0:T(8,128)S(1)} %fusion.42), kind=kOutput, calls=%fused_computation.12 | convolution fusion | flops 7253655552 | bytes 28573696 | tf_op jit(solution)/shard_map/dot_general | solution.py:95
  (74 shorter events, 1.4 us)
Async XLA Ops:
  7.2 292.5 %copy-start = (f32[1024,128]{1,0:T(8,128)S(1)}, f32[1024,128]{1,0:T(8,128)}, u32[]{:S(2)}) copy-start(f32[1024,128]{1,0:T(8,128)} %param.21) | copy-start | bytes 1572868
  7.2 9.2 %copy-start.8 = (f32[48,128]{1,0:T(8,128)S(1)}, f32[48,128]{1,0:T(8,128)}, u32[]{:S(2)}) copy-start(f32[48,128]{1,0:T(8,128)} %param.16) | copy-start | bytes 73732
  7.2 32.6 %copy-start.4 = (f32[192,32]{0,1:T(8,128)S(1)}, f32[192,32]{0,1:T(8,128)}, u32[]{:S(2)}) copy-start(f32[192,32]{0,1:T(8,128)} %param.17) | copy-start | bytes 73732
  7.2 87.2 %copy-start.5 = (f32[192,32]{0,1:T(8,128)S(1)}, f32[192,32]{0,1:T(8,128)}, u32[]{:S(2)}) copy-start(f32[192,32]{0,1:T(8,128)} %param.18) | copy-start | bytes 73732
  7.2 276.9 %all-gather.7.cloned.1.call-start = ((), (), s32[]{:S(2)}) async-start(), calls=%async_computation | async-start | bytes 7077888 | tf_op jit(solution)/shard_map/all_gather | solution.py:10
  11.3 122.6 %copy-start.9 = (f32[128,32]{0,1:T(8,128)S(1)}, f32[128,32]{0,1:T(8,128)}, u32[]{:S(2)}) copy-start(f32[128,32]{0,1:T(8,128)} %param.20) | copy-start | bytes 49156
  285.3 14.4 %copy-start.6 = (f32[48,128]{1,0:T(8,128)S(1)}, f32[48,128]{1,0:T(8,128)}, u32[]{:S(2)}) copy-start(f32[48,128]{1,0:T(8,128)} %param.15) | copy-start | bytes 73732
  285.3 30.9 %copy-start.11 = (f32[128,64]{0,1:T(8,128)S(1)}, f32[128,64]{0,1:T(8,128)}, u32[]{:S(2)}) copy-start(f32[128,64]{0,1:T(8,128)} %param.23) | copy-start | bytes 98308
  285.3 31.1 %copy-start.12 = (f32[128,64]{0,1:T(8,128)S(1)}, f32[128,64]{0,1:T(8,128)}, u32[]{:S(2)}) copy-start(f32[128,64]{0,1:T(8,128)} %param.22) | copy-start | bytes 98308
  285.4 57.1 %copy-start.3 = (f32[128,128]{1,0:T(8,128)S(1)}, f32[128,128]{1,0:T(8,128)}, u32[]{:S(2)}) copy-start(f32[128,128]{1,0:T(8,128)} %param.24) | copy-start | bytes 196612
  299.0 96.3 %slice-start.4 = ((f32[128,128]{1,0:T(8,128)}), f32[64,128]{1,0:T(8,128)S(1)}, s32[]{:S(2)}) async-start(f32[128,128]{1,0:T(8,128)} %param.24), calls=%async_computation.5 | async-start | bytes 65536 | tf_op jit(solution)/shard_map/slice | solution.py:81
  299.0 96.3 %copy-start.10 = (f32[128]{0:T(128)S(1)}, f32[128]{0:T(128)}, u32[]{:S(2)}) copy-start(f32[128]{0:T(128)} %param.25) | copy-start | bytes 1540
  300.2 107.4 %copy-start.7 = (f32[48,128]{1,0:T(8,128)}, f32[48,128]{1,0:T(8,128)S(1)}, u32[]{:S(2)}) copy-start(f32[48,128]{1,0:T(8,128)S(1)} %get-tuple-element.239) | copy-start | bytes 73732
  407.8 6.3 %slice-start.2 = ((s8[4718592]{0:T(1024)(128)(4,1)}), s8[524288]{0:T(1024)(128)(4,1)S(1)}, s32[]{:S(2)}) async-start(s8[4718592]{0:T(1024)(128)(4,1)} %bitcast.63), calls=%async_computation.3 | async-start | bytes 1048576
  407.9 6.2 %slice-start.3 = ((s8[4718592]{0:T(1024)(128)(4,1)}), s8[4194304]{0:T(1024)(128)(4,1)S(1)}, s32[]{:S(2)}) async-start(s8[4718592]{0:T(1024)(128)(4,1)} %bitcast.63), calls=%async_computation.4 | async-start | bytes 8388608
  417.0 7.2 %copy-start.1 = (f32[128,512]{1,0:T(8,128)S(1)}, f32[128,512]{1,0:T(8,128)}, u32[]{:S(2)}) copy-start(f32[128,512]{1,0:T(8,128)} %param.26) | copy-start | bytes 786436
  417.0 23.4 %slice-start = ((s8[4718592]{0:T(1024)(128)(4,1)}), s8[4194304]{0:T(1024)(128)(4,1)S(1)}, s32[]{:S(2)}) async-start(s8[4718592]{0:T(1024)(128)(4,1)} %bitcast.60), calls=%async_computation.1 | async-start | bytes 8388608
  424.1 16.2 %slice-start.1 = ((s8[4718592]{0:T(1024)(128)(4,1)}), s8[524288]{0:T(1024)(128)(4,1)S(1)}, s32[]{:S(2)}) async-start(s8[4718592]{0:T(1024)(128)(4,1)} %bitcast.60), calls=%async_computation.2 | async-start | bytes 1048576
  424.1 16.2 %copy-start.2 = (f32[512,128]{1,0:T(8,128)S(1)}, f32[512,128]{1,0:T(8,128)}, u32[]{:S(2)}) copy-start(f32[512,128]{1,0:T(8,128)} %param.27) | copy-start | bytes 786436
Sparse Core Ops, SparseCore 0:
  152.1 131.9 all-gather.6
where the time goes:
time: 472 us; the launch traced here: 464 us
  blocking collectives  270 us (57%)
  waiting for transfers between devices  72.8 us (15%)
  matrix products  63 us (13%)
  other arithmetic  32 us (7%)
  between operations  14.7 us (3%)
  local copies, waits for them, and re-layouts  11.2 us (2%)
    all_gather x1, waiting for transfers between devices, merged(): everything = jax.tree.map(lambda part: lax.all_gather(part, axis), x)  72.8 us
    all_gather x2, blocking collectives, merged(): everything = jax.tree.map(lambda part: lax.all_gather(part, axis), x)  58.6 us
    all_gather x1, blocking collectives, per_device(): lax.all_gather(key, 'row', axis=1, tiled=True)  54.6 us
    all_gather x1, blocking collectives, per_device(): right_every = lax.all_gather(right, 'row', axis=0, tiled=True)  52.4 us
    all_gather x1, blocking collectives, per_device(): lax.all_gather(value, 'row', axis=1, tiled=True)  39.6 us
    psum x1, blocking collectives, per_device(): left, right = lax.psum((left_part, right_part), 'col')  25.8 us
    all_gather x1, blocking collectives, per_device(): queries = lax.all_gather(query, 'col', axis=1, tiled=True)  23.2 us
    dot_general x1, matrix products, per_device(): pair_new = flat + jnp.dot(hidden_act, w_down, precision=HIGH)  16.7 us
  transfers between devices with their start and end apart: 1, of which 1 were waited for; matrix products, arithmetic and copies ran while one was open for 0% of the time, Pallas kernels for 0%

commit v1 on v0

v1 whole, which is shorter than its diff:
```python
import functools

import jax
import jax.numpy as jnp
from jax import lax
from jax.experimental import pallas as pl
from jax.experimental.pallas import tpu as pltpu
from jax.sharding import PartitionSpec as P

HIGH = lax.Precision.HIGHEST
EPS = 1e-05
BF = jnp.bfloat16
F32 = jnp.float32
ROWS_PER_STEP = 4


def dot(a, b, dims=((1,), (0,)), precision=HIGH):
    return lax.dot_general(a, b, (dims, ((), ())), precision=precision, preferred_element_type=F32)


def bdot(a, b):
    return lax.dot_general(a, b, (((1,), (0,)), ((), ())), preferred_element_type=F32)


def channel_norm(x):
    centre = x - jnp.mean(x, axis=-1, keepdims=True)
    return centre * lax.rsqrt(jnp.mean(centre * centre, axis=-1, keepdims=True) + EPS)


def split(x):
    high = lax.reduce_precision(x, 8, 7)
    return high.astype(BF), (x - high).astype(BF)


def ksplit(x):
    high = x.astype(BF)
    return high, (x - high.astype(F32)).astype(BF)


def merge_kernel(heads_per, parts_ref, out_ref):
    sources, _, lanes = parts_ref.shape
    rows = out_ref.shape[1]
    tops = [parts_ref[s, rows : rows + 8, :] for s in range(sources)]
    top = functools.reduce(jnp.maximum, [t[:heads_per] for t in tops])
    scales = [jnp.exp(t[:heads_per] - top) for t in tops]
    total = sum(t[heads_per : 2 * heads_per] * s for t, s in zip(tops, scales))
    row = lax.broadcasted_iota(jnp.int32, (heads_per, lanes), 0)
    lane = lax.broadcasted_iota(jnp.int32, (heads_per, lanes), 1)
    spread = (lane // (lanes // heads_per) == row).astype(F32)
    attn = jnp.zeros((rows, lanes), F32)
    for s in range(sources):
        factor = dot(scales[s] / total, spread, ((0,), (0,)))
        attn = attn + parts_ref[s, :rows, :] * factor[:rows]
    for s in range(sources):
        out_ref[s] = attn


def project_kernel(attn_ref, w_out_ref, seq_ref, w_lr_ref, seq_new_ref, out_ref):
    sources, rows, lanes = attn_ref.shape
    total = seq_ref[...]
    for s in range(sources):
        total = total + dot(attn_ref[s], w_out_ref[s * lanes : (s + 1) * lanes, :])
    seq_new_ref[...] = total
    w_lr = w_lr_ref[...]
    part = dot(total, w_lr)
    ones = jnp.ones((8, lanes), F32)
    sums = dot(ones, total, ((1,), (1,)))
    squares = dot(ones, total * total, ((1,), (1,)))
    row = lax.broadcasted_iota(jnp.int32, (8, rows), 0)
    stats = jnp.where(row == 0, sums, squares)
    columns = jnp.sum(w_lr, axis=0, keepdims=True)
    for s in range(out_ref.shape[0]):
        out_ref[s, :rows, :] = part
        out_ref[s, rows : rows + 8, :] = jnp.zeros((8, lanes), F32)
        out_ref[s, rows : rows + 2, :rows] = stats[:2]
        out_ref[s, rows + 2 : rows + 3, :] = columns


def left_right_kernel(width, parts_ref, left_ref, right_ref):
    sources = parts_ref.shape[0]
    rows, lanes = left_ref.shape
    total = parts_ref[0]
    for s in range(1, sources):
        total = total + parts_ref[s]
    stats = jnp.transpose(total[rows : rows + 8, :])
    mean = stats[:rows, 0:1] / width
    square = stats[:rows, 1:2] / width
    both = (total[:rows] - mean * total[rows + 2 : rows + 3]) * lax.rsqrt(square - mean * mean + EPS)
    swapped = pltpu.roll(both, lanes // 2, 1)
    first = lax.broadcasted_iota(jnp.int32, (rows, lanes), 1) < lanes // 2
    left_ref[...] = jnp.where(first, both, swapped)
    right = jnp.where(first, swapped, both)
    packed = jnp.where(first[: rows // 2], right[: rows // 2], right[rows // 2 :])
    for s in range(right_ref.shape[0]):
        right_ref[s] = packed


def update_kernel(
    pair_ref, left_ref, right_ref, w_diff_ref, bias_ref, w_prod_ref, w_up_ref, w_down_ref, out_ref,
    rights, base, diffs,
):
    step = pl.program_id(0)
    lanes = pair_ref.shape[2]

    @pl.when(step == 0)
    def _():
        w_diff = w_diff_ref[...]
        half = right_ref.shape[1]
        first = lax.broadcasted_iota(jnp.int32, (half, lanes), 1) < lanes // 2
        for block in range(right_ref.shape[0]):
            packed = right_ref[block]
            swapped = pltpu.roll(packed, lanes // 2, 1)
            start = 2 * half * block
            rights[start : start + half, :] = jnp.where(first, packed, swapped)
            rights[start + half : start + 2 * half, :] = jnp.where(first, swapped, packed)
        base[...] = bias_ref[...] - dot(rights[:, : lanes // 2], w_diff)
        diffs[...] = dot(left_ref[:, : lanes // 2], w_diff)

    first = lax.broadcasted_iota(jnp.int32, base.shape, 1) < lanes // 2
    for r in range(ROWS_PER_STEP):
        i = step * ROWS_PER_STEP + r
        product = rights[...] * left_ref[pl.ds(i, 1), :]
        high = product.astype(BF).astype(F32)
        both = jnp.where(first, high, product - high).astype(BF)
        mid = (
            pair_ref[r]
            + bdot(jnp.concatenate([both, both], axis=1), w_prod_ref[...])
            + (base[...] + diffs[pl.ds(i, 1), :])
        )
        n_high, n_low = ksplit(channel_norm(mid))
        up = bdot(jnp.concatenate([n_high, n_low, n_high, n_low], axis=1), w_up_ref[...])
        h_high, h_low = ksplit(jnp.maximum(up, 0.0))
        down = bdot(jnp.concatenate([h_high, h_low], axis=1), w_down_ref[...])
        out_ref[r] = mid + (down[:, :lanes] + down[:, lanes:])


def update_pair(pair, left, right, w_outer, outer_bias, w_up, w_down):
    rows, cols, channels = pair.shape
    proj = w_outer.shape[0] // 2
    hidden = w_up.shape[1]
    p_high, p_low = split(w_outer[:proj])
    u_high, u_low = split(w_up)
    d_high, d_low = split(w_down)
    w_prod = jnp.concatenate([p_high, p_high, p_low, p_low], axis=0)
    w_up4 = jnp.concatenate([u_high, u_high, u_low, u_low], axis=0)
    d_both = jnp.concatenate([d_high, d_low], axis=1)
    w_down4 = jnp.concatenate([d_both, d_both], axis=0)
    whole = lambda x: pl.BlockSpec(x.shape, lambda s: (0,) * x.ndim)
    block = pl.BlockSpec((ROWS_PER_STEP, cols, channels), lambda s: (s, 0, 0))
    fixed = (left, right, w_outer[proj:], outer_bias[None, :], w_prod, w_up4, w_down4)
    cells = rows * cols
    return pl.pallas_call(
        update_kernel,
        grid=(rows // ROWS_PER_STEP,),
        in_specs=[block] + [whole(x) for x in fixed],
        out_specs=block,
        out_shape=jax.ShapeDtypeStruct(pair.shape, F32),
        scratch_shapes=[
            pltpu.VMEM((cols, channels), F32),
            pltpu.VMEM((cols, channels), F32),
            pltpu.VMEM((rows, channels), F32),
        ],
        compiler_params=pltpu.CompilerParams(vmem_limit_bytes=40 * 2**20),
        cost_estimate=pl.CostEstimate(
            flops=2 * cells * channels * (4 * hidden + 4 * hidden + 256),
            bytes_accessed=8 * cells * channels,
            transcendentals=cells,
        ),
        name="update_pair",
    )(pair, *fixed)


def spread_to(x, axis):
    return lax.all_to_all(jnp.broadcast_to(x, (lax.axis_size(axis),) + x.shape), axis, 0, 0)


def per_device(
    seq, query, key, value, pair, w_bias, w_out, w_left, w_right, w_outer, outer_bias, w_up, w_down
):
    rows, cols, channels = pair.shape
    heads = w_bias.shape[1]
    width = w_out.shape[0]
    head_dim = width // heads
    n_row, n_col = lax.axis_size("row"), lax.axis_size("col")
    group = heads // n_col
    scale = 1.0 / jnp.sqrt(jnp.float32(head_dim))

    half = cols // 2
    own = jnp.concatenate([key[:half], value[:half], key[half:], value[half:]], axis=1)
    pairs = [[z * 2 + k for z in range(n_row // 2)] for k in range(2)]
    across = lax.all_to_all(
        jnp.broadcast_to(own, (n_row // 2,) + own.shape), "row", 0, 0, axis_index_groups=pairs
    )
    other = lax.ppermute(across, "row", [(i, i ^ 1) for i in range(n_row)])
    even = (lax.axis_index("row") % 2 == 0)
    kv = jnp.where(even, jnp.stack([across, other], 1), jnp.stack([other, across], 1))
    kv = kv.reshape(heads, half, 2, 2, head_dim).transpose(3, 0, 2, 1, 4)
    keys = kv[0].reshape(heads, cols, head_dim)
    values = kv[1].reshape(heads, cols, head_dim)
    queries = spread_to(query, "col").reshape(n_col, rows, group, head_dim)
    queries = queries.transpose(0, 2, 1, 3).reshape(heads, rows, head_dim)

    bias = jnp.einsum("ijc,ch->hij", channel_norm(pair), w_bias, precision=HIGH)
    scores = jnp.einsum("hid,hjd->hij", queries, keys, precision=HIGH) * scale + bias
    top = jnp.max(scores, axis=2)
    expo = jnp.exp(scores - top[..., None])
    totals = jnp.sum(expo, axis=2)
    weighted = jnp.einsum("hij,hjd->hid", expo, values, precision=HIGH)

    stats = jnp.concatenate([top.reshape(n_col, group, rows), totals.reshape(n_col, group, rows)], axis=1)
    stats = jnp.pad(stats, ((0, 0), (0, 0), (0, channels - rows)))
    shares = weighted.reshape(n_col, group, rows, head_dim).transpose(0, 2, 1, 3).reshape(n_col, rows, channels)
    parts = lax.all_to_all(jnp.concatenate([shares, stats], axis=1), "col", 0, 0)

    attn = pl.pallas_call(
        functools.partial(merge_kernel, group),
        out_shape=jax.ShapeDtypeStruct((n_col, rows, channels), F32),
        name="merge",
    )(parts)
    attn = lax.all_to_all(attn, "col", 0, 0)
    seq_new, shares = pl.pallas_call(
        project_kernel,
        out_shape=(
            jax.ShapeDtypeStruct(seq.shape, F32),
            jax.ShapeDtypeStruct((n_col, rows + 8, channels), F32),
        ),
        name="project",
    )(attn, w_out, seq, jnp.concatenate([w_left, w_right], axis=1))
    shares = lax.all_to_all(shares, "col", 0, 0)
    left, right = pl.pallas_call(
        functools.partial(left_right_kernel, width),
        out_shape=(
            jax.ShapeDtypeStruct((rows, channels), F32),
            jax.ShapeDtypeStruct((n_row, rows // 2, channels), F32),
        ),
        name="left_right",
    )(shares)
    every = lax.all_to_all(right, "row", 0, 0)
    blocks = cols // rows
    mine = lax.dynamic_slice_in_dim(every, lax.axis_index("col") * blocks, blocks, 0)
    return seq_new, update_pair(pair, left, mine, w_outer, outer_bias, w_up, w_down)


def solution(mesh):
    in_specs = (
        P("row", "col"),
        P("row", "col"),
        P("col", "row"),
        P("col", "row"),
        P("row", "col", None),
        P(),
        P(None, "col"),
        P("col", None),
        P("col", None),
        P(),
        P(),
        P(),
        P(),
    )
    out_specs = (P("row", "col"), P("row", "col", None))
    return jax.shard_map(
        per_device, mesh=mesh, in_specs=in_specs, out_specs=out_specs, check_vma=False
    )
```

time: 472 us -> 171 us (0.36); the launches traced: 464 us -> 170 us
  blocking collectives: 270 us -> 11.7 us
  matrix products: 63 us -> 16.3 us
  Pallas kernels: 0 us -> 36.5 us
  waiting for transfers between devices: 72.8 us -> 37.5 us
  starting transfers between devices: 0.04 us -> 33.3 us
  other arithmetic: 32 us -> 13.2 us
  between operations: 14.7 us -> 1 us
  local copies, waits for them, and re-layouts: 11.2 us -> 20.4 us
    all_gather x6 -> x0, blocking collectives: 228 us -> none  [the longest x2 58.6 us: merged(): everything = jax.tree.map(lambda part: lax.all_gather(part, axis), x)]
    all_gather x1 -> x0, waiting for transfers between devices: 72.8 us -> none  [merged(): everything = jax.tree.map(lambda part: lax.all_gather(part, axis), x)]
    dot_general x11 -> x3, matrix products: 63 us -> 16.3 us  [the longest x1 12.2 us: per_device(): bias = jnp.einsum('ijc,ch->hij', channel_norm(pair), w_bias, precision=HIGH)]
    psum x2 -> x0, blocking collectives: 41.7 us -> none  [the longest x1 25.8 us: per_device(): left, right = lax.psum((left_part, right_part), 'col')]
    all_to_all x0 -> x5, waiting for transfers between devices: none -> 37.5 us  [the longest x1 14.1 us: per_device(): every = lax.all_to_all(right, 'row', 0, 0)]
    pallas_call x0 -> x4, Pallas kernels: none -> 36.5 us  [the longest x1 29.5 us: update_pair(): pl.pallas_call(update_kernel, grid=(rows // ROWS_PER_STEP,), in_specs=[bl...]
    all_to_all x0 -> x5, starting transfers between devices: none -> 30 us  [the longest x1 11.7 us: per_device(): lax.all_to_all(jnp.broadcast_to(own, (n_row // 2,) + own.shape), 'row', 0...]
    add x14 -> x0, other arithmetic: 12.2 us -> none  [the longest x7 12 us: combine(): first[2] * scale_one[..., None] + second[2] * scale_two[..., None]]
  transfers between devices with their start and end apart: 1 -> 6, of which waited for: 1 -> 4; matrix products, arithmetic and copies ran while one was open for 0% -> 14% of each run, Pallas kernels for 0% -> 0%
where the time goes in v1:
time: 171 us; the launch traced here: 170 us
  waiting for transfers between devices  37.5 us (22%)
  Pallas kernels  36.5 us (21%)
  starting transfers between devices  33.3 us (19%)
  local copies, waits for them, and re-layouts  20.4 us (12%)
  matrix products  16.3 us (10%)
  other arithmetic  13.2 us (8%)
  blocking collectives  11.7 us (7%)
    pallas_call x1, Pallas kernels, update_pair(): pl.pallas_call(update_kernel, grid=(rows // ROWS_PER_STEP,), in_specs=[bl...  29.5 us
    all_to_all x1, waiting for transfers between devices, per_device(): every = lax.all_to_all(right, 'row', 0, 0)  14.1 us
    all_to_all x1, waiting for transfers between devices, per_device(): lax.all_to_all(jnp.broadcast_to(own, (n_row // 2,) + own.shape), 'row', 0...  13.3 us
    dot_general x1, matrix products, per_device(): bias = jnp.einsum('ijc,ch->hij', channel_norm(pair), w_bias, precision=HIGH)  12.2 us
    all_to_all x1, starting transfers between devices, per_device(): lax.all_to_all(jnp.broadcast_to(own, (n_row // 2,) + own.shape), 'row', 0...  11.7 us
    all_to_all x1, blocking collectives, per_device(): lax.all_to_all(jnp.concatenate([shares, stats], axis=1), 'col', 0, 0)  11.7 us
    all_to_all x1, starting transfers between devices, per_device(): every = lax.all_to_all(right, 'row', 0, 0)  7.28 us
    all_to_all x1, waiting for transfers between devices, per_device(): shares = lax.all_to_all(shares, 'col', 0, 0)  5.56 us
  transfers between devices with their start and end apart: 6, of which 4 were waited for; matrix products, arithmetic and copies ran while one was open for 14% of the time, Pallas kernels for 0%

profile of v1, /device:TPU:1, one launch (start us, length us, event | category | flops | bytes accessed | tf_op | source)
XLA Modules:
  0.0 170.1 jit_solution(14427824344691190262)
XLA Ops:
  0.6 0.0 copy-start
  0.6 0.9 fusion.14
  1.5 0.1 copy.55
  1.6 1.0 broadcast_in_dim.13
  2.6 11.7 %all-to-all-start.1 = ((f32[16,96,128]{2,1,0:T(8,128)}), f32[16,96,128]{2,1,0:T(8,128)S(1)}, u32[]{:S(2)}, u32[]{:S(2)}) async-start(f32[16,96,128]{2,1,0:T(8,128)} %broadcast_in_dim.13), calls=%async_computation.1 | async-start | bytes 1572864 | tf_op jit(solution)/shard_map/all_to_all | solution.py:191
  14.3 4.0 %reduce_sum.27 = f32[48,192]{1,0:T(8,128)S(1)} reduce(f32[48,192,128]{2,1,0:T(8,128)} %pair_ref.1, f32[]{:T(128)} %constant.33.clone.1), dimensions={2}, to_apply=%region_0.1 | reduce | flops 1170432 | bytes 4755460 | tf_op jit(solution)/shard_map/reduce_sum | solution.py:26
  18.4 0.0 copy-start.13
  18.4 4.9 %multiply_reduce_fusion = f32[48,192]{1,0:T(8,128)S(1)} fusion(f32[48,192,128]{2,1,0:T(8,128)} %pair_ref.1, f32[48,192]{1,0:T(8,128)S(1)} %broadcast_multiply_fusion), kind=kLoop, calls=%fused_computation.2 | loop fusion | flops 3529728 | bytes 4792320 | tf_op jit(solution)/shard_map/reduce_sum | solution.py:27
  23.3 13.3 %all-to-all-done.1 = f32[16,96,128]{2,1,0:T(8,128)S(1)} async-done(((f32[16,96,128]{2,1,0:T(8,128)}), f32[16,96,128]{2,1,0:T(8,128)S(1)}, u32[]{:S(2)}, u32[]{:S(2)}) %all-to-all-start.1) | async-done | bytes 786464 | tf_op jit(solution)/shard_map/all_to_all | solution.py:191
  36.6 0.7 broadcast_in_dim.12
  37.3 4.1 %all-to-all-start = ((f32[8,48,128]{2,1,0:T(8,128)}), f32[8,48,128]{2,1,0:T(8,128)S(1)}, u32[]{:S(2)}, u32[]{:S(2)}) async-start(f32[8,48,128]{2,1,0:T(8,128)} %broadcast_in_dim.12), calls=%async_computation | async-start | bytes 393216 | tf_op jit(solution)/shard_map/all_to_all | solution.py:174
  41.5 3.4 %collective-permute-start = (f32[16,96,128]{2,1,0:T(8,128)S(1)}, f32[16,96,128]{2,1,0:T(8,128)}, u32[]{:S(2)}, u32[]{:S(2)}) collective-permute-start(f32[16,96,128]{2,1,0:T(8,128)S(1)} %all-to-all-done.1), channel_id=1, source_target_pairs={{0,8},{8,0},{16,24},{24,16},{32,40},{40,32},{48,56},{56,48},{64,72... | collective-permute-start | bytes 2359304 | tf_op jit(solution)/shard_map/ppermute | solution.py:194
  44.9 12.2 %fusion = f32[48,192,32]{1,2,0:T(8,128)S(1)} fusion(f32[48,192,128]{2,1,0:T(8,128)} %pair_ref.1, f32[48,192]{1,0:T(8,128)S(1)} %add_rsqrt_fusion, f32[48,192]{1,0:T(8,128)S(1)} %broadcast_multiply_fusion, f32[128,32]{0,1:T(8,128)S(1)} %copy-done), kind=kOutput, calls=%fused_computation | convolution fusion | flops 455344128 | bytes 5988352 | tf_op jit(solution)/shard_map/ijc,ch->hij/dot_general | solution.py:203
  57.1 0.2 fusion.13
  57.3 1.0 pad_maximum_fusion
  58.3 0.3 copy.56
  58.6 2.4 %copy.57 = f32[16,96,128]{1,2,0:T(8,128)} copy(f32[16,96,128]{2,1,0:T(8,128)} %collective-permute-done) | data formatting | bytes 1572864 | tf_op jit(solution)/shard_map/ppermute | solution.py:194
  61.1 1.8 %maximum_select_fusion = f32[16,2,96,128]{2,3,1,0:T(8,128)S(1)} fusion(f32[16,1,96,128]{2,3,1,0:T(8,128)} %bitcast.29, f32[16,1,96,128]{2,3,1,0:T(8,128)S(1)} %bitcast.28, pred[]{:T(512)S(6)} %eq.5), kind=kLoop, calls=%fused_computation.6 | loop fusion | flops 1179648 | bytes 3145729 | tf_op jit(solution)/shard_map/jit(_where)/select_n | solution.py:196
  62.9 1.1 fusion.12
  64.0 1.8 %copy.58 = f32[1,32,2,96,32]{3,2,4,1,0:T(2,128)} copy(f32[1,32,2,96,32]{3,4,0,2,1:T(8,128)S(1)} %get-tuple-element.11) | data formatting | bytes 1572864 | tf_op jit(solution)/shard_map/slice | solution.py:198
  65.8 1.8 %reshape_squeeze.6 = f32[32,192,32]{1,2,0:T(8,128)S(1)} reshape(f32[1,32,2,96,32]{3,2,4,1,0:T(2,128)} %copy.58) | data formatting | bytes 1572864 | tf_op jit(solution)/shard_map/reshape;squeeze | solution.py:198
  67.7 3.1 %copy.61 = f32[1,32,2,96,32]{3,2,4,1,0:T(2,128)} copy(f32[1,32,2,96,32]{3,4,0,2,1:T(8,128)} %get-tuple-element.10) | data formatting | bytes 1572864 | tf_op jit(solution)/shard_map/slice | solution.py:199
  70.8 2.8 %reshape_squeeze.7 = f32[32,192,32]{1,2,0:T(8,128)} reshape(f32[1,32,2,96,32]{3,2,4,1,0:T(2,128)} %copy.61) | data formatting | bytes 1572864 | tf_op jit(solution)/shard_map/reshape;squeeze | solution.py:199
  73.6 2.4 %fusion.16 = (f32[32,48]{1,0:T(8,128)S(1)}, f32[32,48,192]{2,1,0:T(8,128)S(1)}) fusion(f32[48,192,32]{1,2,0:T(8,128)S(1)} %fusion, f32[32,48,32]{2,1,0:T(8,128)S(1)} %bitcast.30, f32[32,192,32]{1,2,0:T(8,128)S(1)} %reshape_squeeze.6), kind=kOutput, calls=%fused_computation.38 | convolution fusion | flops 114129408 | bytes 3348480 | tf_op jit(solution)/shard_map/hid,hjd->hij/dot_general | solution.py:204
  76.0 0.5 fusion.5
  76.5 0.0 copy-start.11
  76.5 1.8 %fusion.6 = f32[32,48,32]{1,2,0:T(8,128)S(1)} fusion(f32[32,192,32]{1,2,0:T(8,128)S(1)} %copy-done.4, f32[32,48,192]{2,1,0:T(8,128)S(1)} %get-tuple-element.28, f32[32,48]{1,0:T(8,128)S(1)} %get-tuple-element.27), kind=kOutput, calls=%fused_computation.10 | convolution fusion | flops 113541120 | bytes 2168832 | tf_op jit(solution)/shard_map/hij,hjd->hid/dot_general | solution.py:208
  78.3 0.0 copy-start.12
  78.3 0.0 copy-start.10
  78.3 0.2 copy.62
  78.6 0.0 copy-start.8
  78.6 11.7 %all_to_all.30.parts_ref = f32[8,56,128]{2,1,0:T(8,128)} all-to-all(f32[8,56,128]{2,1,0:T(8,128)S(1)} %pad_maximum_fusion.2), channel_id=1, replica_groups=mesh['row'=32,'col'=8] {'col'}, dimensions={0} | all-to-all | bytes 458752 | tf_op jit(solution)/shard_map/all_to_all | solution.py:213
  90.3 2.3 %merge.1 = f32[8,48,128]{2,1,0:T(8,128)} custom-call(f32[8,56,128]{2,1,0:T(8,128)} %all_to_all.30.parts_ref), custom_call_target="tpu_custom_call" | custom-call | tf_op jit(solution)/shard_map/merge/pallas_call | solution.py:215
  92.6 3.4 %all-to-all-start.3 = ((f32[8,48,128]{2,1,0:T(8,128)}), f32[8,48,128]{2,1,0:T(8,128)S(1)}, u32[]{:S(2)}, u32[]{:S(2)}) async-start(f32[8,48,128]{2,1,0:T(8,128)} %merge.1), calls=%async_computation.3 | async-start | bytes 393216 | tf_op jit(solution)/shard_map/all_to_all | solution.py:220
  96.0 0.1 copy.63
  96.1 0.1 copy.64
  96.2 0.7 pad_maximum_fusion.4.w_lr_ref
  96.9 4.5 %all-to-all-done.3.attn_ref = f32[8,48,128]{2,1,0:T(8,128)S(1)} async-done(((f32[8,48,128]{2,1,0:T(8,128)}), f32[8,48,128]{2,1,0:T(8,128)S(1)}, u32[]{:S(2)}, u32[]{:S(2)}) %all-to-all-start.3) | async-done | bytes 196640 | tf_op jit(solution)/shard_map/all_to_all | solution.py:220
  101.5 0.7 copy-done.7
  102.1 2.8 %project.1 = (f32[48,128]{1,0:T(8,128)}, f32[8,56,128]{2,1,0:T(8,128)}) custom-call(f32[8,48,128]{2,1,0:T(8,128)} %copy-done.7, f32[1024,128]{1,0:T(8,128)} %w_out_ref.1, f32[48,128]{1,0:T(8,128)} %seq_ref.1, f32[128,128]{1,0:T(8,128)} %pad_maximum_fusion.4.w_lr_ref), custom_call_target="tpu_custom_call" | custom-call | tf_op jit(solution)/shard_map/project/pallas_call | solution.py:221
  104.9 3.4 %all-to-all-start.4 = ((f32[8,56,128]{2,1,0:T(8,128)}), f32[8,56,128]{2,1,0:T(8,128)S(1)}, u32[]{:S(2)}, u32[]{:S(2)}) async-start(f32[8,56,128]{2,1,0:T(8,128)} %get-tuple-element.7), calls=%async_computation.4 | async-start | bytes 458752 | tf_op jit(solution)/shard_map/all_to_all | solution.py:229
  108.3 5.6 %all-to-all-done.4.parts_ref = f32[8,56,128]{2,1,0:T(8,128)S(1)} async-done(((f32[8,56,128]{2,1,0:T(8,128)}), f32[8,56,128]{2,1,0:T(8,128)S(1)}, u32[]{:S(2)}, u32[]{:S(2)}) %all-to-all-start.4) | async-done | bytes 229408 | tf_op jit(solution)/shard_map/all_to_all | solution.py:229
  113.9 0.7 copy-done.6
  114.6 2.0 %left_right.1 = (f32[48,128]{1,0:T(8,128)}, f32[32,24,128]{2,1,0:T(8,128)}) custom-call(f32[8,56,128]{2,1,0:T(8,128)} %copy-done.6), custom_call_target="tpu_custom_call" | custom-call | tf_op jit(solution)/shard_map/left_right/pallas_call | solution.py:230
  116.6 7.3 %all-to-all-start.5 = ((f32[32,24,128]{2,1,0:T(8,128)}), f32[32,24,128]{2,1,0:T(8,128)S(1)}, u32[]{:S(2)}, u32[]{:S(2)}) async-start(f32[32,24,128]{2,1,0:T(8,128)} %get-tuple-element.9), calls=%async_computation.5 | async-start | bytes 786432 | tf_op jit(solution)/shard_map/all_to_all | solution.py:238
  124.1 14.1 %all-to-all-done.5 = f32[32,24,128]{2,1,0:T(8,128)S(1)} async-done(((f32[32,24,128]{2,1,0:T(8,128)}), f32[32,24,128]{2,1,0:T(8,128)S(1)}, u32[]{:S(2)}, u32[]{:S(2)}) %all-to-all-start.5) | async-done | bytes 393248 | tf_op jit(solution)/shard_map/all_to_all | solution.py:238
  138.3 2.3 %copy-done.1 = f32[48,192,128]{2,1,0:T(8,128)S(1)} copy-done((f32[48,192,128]{2,1,0:T(8,128)S(1)}, f32[48,192,128]{2,1,0:T(8,128)}, u32[]{:S(2)}) %copy-start.1) | copy-done | bytes 4718616
  140.6 29.5 %update_pair.1 = f32[48,192,128]{2,1,0:T(8,128)} custom-call(f32[48,192,128]{2,1,0:T(8,128)S(1)} %copy-done.1, f32[48,128]{1,0:T(8,128)S(1)} %copy-done.2, f32[4,24,128]{2,1,0:T(8,128)S(1)} %constant_dynamic-slice_fusion.right_ref, f32[64,128]{1,0:T(8,128)S(1)} %get-tuple-element.22.w_diff_ref, f32[1,128]{1,0:T(1,128)S(1)} %bitcast.26, ...), custom_call_target="tpu_custom_call" | custom-call | flops 10267656192 | bytes 9437184 | tf_op jit(solution)/shard_map/update_pair/pallas_call | solution.py:152
  (33 shorter events, 0.3 us)
Async XLA Ops:
  0.6 44.2 %copy-start = (f32[128,32]{0,1:T(8,128)S(1)}, f32[128,32]{0,1:T(8,128)}, u32[]{:S(2)}) copy-start(f32[128,32]{0,1:T(8,128)} %param.18) | copy-start | bytes 49156
  2.6 34.1 %all-to-all-start.1 = ((f32[16,96,128]{2,1,0:T(8,128)}), f32[16,96,128]{2,1,0:T(8,128)S(1)}, u32[]{:S(2)}, u32[]{:S(2)}) async-start(f32[16,96,128]{2,1,0:T(8,128)} %broadcast_in_dim.13), calls=%async_computation.1 | async-start | bytes 1572864 | tf_op jit(solution)/shard_map/all_to_all | solution.py:191
  18.4 18.3 %copy-start.13 = (f32[48,128]{1,0:T(8,128)S(1)}, f32[48,128]{1,0:T(8,128)}, u32[]{:S(2)}) copy-start(f32[48,128]{1,0:T(8,128)} %param.14) | copy-start | bytes 73732
  37.3 19.7 %all-to-all-start = ((f32[8,48,128]{2,1,0:T(8,128)}), f32[8,48,128]{2,1,0:T(8,128)S(1)}, u32[]{:S(2)}, u32[]{:S(2)}) async-start(f32[8,48,128]{2,1,0:T(8,128)} %broadcast_in_dim.12), calls=%async_computation | async-start | bytes 393216 | tf_op jit(solution)/shard_map/all_to_all | solution.py:174
  41.5 17.1 %collective-permute-start = (f32[16,96,128]{2,1,0:T(8,128)S(1)}, f32[16,96,128]{2,1,0:T(8,128)}, u32[]{:S(2)}, u32[]{:S(2)}) collective-permute-start(f32[16,96,128]{2,1,0:T(8,128)S(1)} %all-to-all-done.1), channel_id=1, source_target_pairs={{0,8},{8,0},{16,24},{24,16},{32,40},{40,32},{48,56},{56,48},{64,72... | collective-permute-start | bytes 2359304 | tf_op jit(solution)/shard_map/ppermute | solution.py:194
  67.7 6.0 %copy-start.5 = (f32[8,192,32]{2,1,0:T(8,128)S(1)}, f32[8,192,32]{2,1,0:T(8,128)}, u32[]{:S(2)}) copy-start(f32[8,192,32]{2,1,0:T(8,128)} %pad_maximum_fusion) | copy-start | bytes 589828
  73.6 2.9 %copy-start.4 = (f32[32,192,32]{1,2,0:T(8,128)S(1)}, f32[32,192,32]{1,2,0:T(8,128)}, u32[]{:S(2)}) copy-start(f32[32,192,32]{1,2,0:T(8,128)} %reshape_squeeze.7) | copy-start | bytes 2359300
  76.5 19.5 %copy-start.11 = (f32[128,64]{0,1:T(8,128)S(1)}, f32[128,64]{0,1:T(8,128)}, u32[]{:S(2)}) copy-start(f32[128,64]{0,1:T(8,128)} %param.20) | copy-start | bytes 98308
  78.3 17.8 %copy-start.12 = (f32[128,64]{0,1:T(8,128)S(1)}, f32[128,64]{0,1:T(8,128)}, u32[]{:S(2)}) copy-start(f32[128,64]{0,1:T(8,128)} %param.21) | copy-start | bytes 98308
  78.3 30.0 %copy-start.10 = (f32[128,128]{1,0:T(8,128)S(1)}, f32[128,128]{1,0:T(8,128)}, u32[]{:S(2)}) copy-start(f32[128,128]{1,0:T(8,128)} %param.22) | copy-start | bytes 196612
  78.6 45.4 %copy-start.8 = (f32[512,128]{1,0:T(8,128)S(1)}, f32[512,128]{1,0:T(8,128)}, u32[]{:S(2)}) copy-start(f32[512,128]{1,0:T(8,128)} %param.25) | copy-start | bytes 786436
  92.6 8.9 %all-to-all-start.3 = ((f32[8,48,128]{2,1,0:T(8,128)}), f32[8,48,128]{2,1,0:T(8,128)S(1)}, u32[]{:S(2)}, u32[]{:S(2)}) async-start(f32[8,48,128]{2,1,0:T(8,128)} %merge.1), calls=%async_computation.3 | async-start | bytes 393216 | tf_op jit(solution)/shard_map/all_to_all | solution.py:220
  96.0 28.0 %copy-start.9 = (f32[128,512]{1,0:T(8,128)S(1)}, f32[128,512]{1,0:T(8,128)}, u32[]{:S(2)}) copy-start(f32[128,512]{1,0:T(8,128)} %param.24) | copy-start | bytes 786436
  101.5 0.7 copy-start.7
  104.9 9.0 %all-to-all-start.4 = ((f32[8,56,128]{2,1,0:T(8,128)}), f32[8,56,128]{2,1,0:T(8,128)S(1)}, u32[]{:S(2)}, u32[]{:S(2)}) async-start(f32[8,56,128]{2,1,0:T(8,128)} %get-tuple-element.7), calls=%async_computation.4 | async-start | bytes 458752 | tf_op jit(solution)/shard_map/all_to_all | solution.py:229
  108.3 29.9 %copy-start.3 = (f32[128]{0:T(128)S(1)}, f32[128]{0:T(128)}, u32[]{:S(2)}) copy-start(f32[128]{0:T(128)} %param.23) | copy-start | bytes 1540
  113.9 0.7 copy-start.6
  116.6 21.6 %copy-start.2 = (f32[48,128]{1,0:T(8,128)S(1)}, f32[48,128]{1,0:T(8,128)}, u32[]{:S(2)}) copy-start(f32[48,128]{1,0:T(8,128)} %get-tuple-element.8.left_ref) | copy-start | bytes 73732
  116.6 21.6 %all-to-all-start.5 = ((f32[32,24,128]{2,1,0:T(8,128)}), f32[32,24,128]{2,1,0:T(8,128)S(1)}, u32[]{:S(2)}, u32[]{:S(2)}) async-start(f32[32,24,128]{2,1,0:T(8,128)} %get-tuple-element.9), calls=%async_computation.5 | async-start | bytes 786432 | tf_op jit(solution)/shard_map/all_to_all | solution.py:238
  138.3 2.3 %copy-start.1 = (f32[48,192,128]{2,1,0:T(8,128)S(1)}, f32[48,192,128]{2,1,0:T(8,128)}, u32[]{:S(2)}) copy-start(f32[48,192,128]{2,1,0:T(8,128)} %pair_ref.1) | copy-start | bytes 14155780

commit v2 on v1

v2 whole, which is shorter than its diff:
```python
import functools

import jax
import jax.numpy as jnp
from jax import lax
from jax.experimental import pallas as pl
from jax.experimental.pallas import tpu as pltpu
from jax.sharding import PartitionSpec as P

HIGH = lax.Precision.HIGHEST
EPS = 1e-05
BF = jnp.bfloat16
F32 = jnp.float32
BIAS_ROWS = 16
ATTENTION_GROUPS = 4
UPDATE_ROWS = 24
CHUNK_ROWS = 4
MIB = 2**20


def dot(a, b, dims=((1,), (0,)), precision=HIGH):
    return lax.dot_general(a, b, (dims, ((), ())), precision=precision, preferred_element_type=F32)


def bdot(a, b, dims=((1,), (0,))):
    return lax.dot_general(a, b, (dims, ((), ())), preferred_element_type=F32)


def channel_norm(x):
    centre = x - jnp.mean(x, axis=-1, keepdims=True)
    return centre * lax.rsqrt(jnp.mean(centre * centre, axis=-1, keepdims=True) + EPS)


def split(x):
    high = lax.reduce_precision(x, 8, 7)
    return high.astype(BF), (x - high).astype(BF)


def ksplit(x):
    high = x.astype(BF)
    return high, (x - high.astype(F32)).astype(BF)


def merge_kernel(group, parts_ref, out_ref):
    sources, _, lanes = parts_ref.shape
    rows = out_ref.shape[1]
    tops = [parts_ref[s, rows : rows + group, :] for s in range(sources)]
    top = functools.reduce(jnp.maximum, tops)
    scales = [jnp.exp(t - top) for t in tops]
    total = sum(parts_ref[s, rows + group :, :] * scales[s] for s in range(sources))
    factors = jnp.concatenate([x / total for x in scales], axis=0)
    factors = jnp.concatenate([factors, jnp.zeros((lanes - sources * group, lanes), F32)], axis=0)
    factors = jnp.transpose(factors)[:rows]
    head = lax.broadcasted_iota(jnp.int32, (rows, lanes), 1) // (lanes // group)
    attn = jnp.zeros((rows, lanes), F32)
    for s in range(sources):
        factor = factors[:, s * group : s * group + 1]
        for h in range(1, group):
            factor = jnp.where(head == h, factors[:, s * group + h : s * group + h + 1], factor)
        attn = attn + parts_ref[s, :rows, :] * factor
    for s in range(sources):
        out_ref[s] = attn


def project_kernel(attn_ref, w_out_ref, seq_ref, w_lr_ref, seq_new_ref, out_ref):
    sources, rows, lanes = attn_ref.shape
    attn = jnp.concatenate([attn_ref[s] for s in range(sources)], axis=1)
    both = bdot(jnp.concatenate(ksplit(attn), axis=0), w_out_ref[...])
    both = both[:, :lanes] + both[:, lanes:]
    total = seq_ref[...] + (both[:rows] + both[rows:])
    seq_new_ref[...] = total
    w_lr = w_lr_ref[...]
    part = dot(total, w_lr)
    ones = jnp.ones((8, lanes), F32)
    sums = dot(ones, total, ((1,), (1,)))
    squares = dot(ones, total * total, ((1,), (1,)))
    row = lax.broadcasted_iota(jnp.int32, (8, rows), 0)
    stats = jnp.where(row == 0, sums, squares)
    columns = jnp.sum(w_lr, axis=0, keepdims=True)
    for s in range(out_ref.shape[0]):
        out_ref[s, :rows, :] = part
        out_ref[s, rows : rows + 8, :] = jnp.zeros((8, lanes), F32)
        out_ref[s, rows : rows + 2, :rows] = stats[:2]
        out_ref[s, rows + 2 : rows + 3, :] = columns


def left_right_kernel(width, parts_ref, left_ref, right_ref):
    sources = parts_ref.shape[0]
    rows, lanes = left_ref.shape
    total = parts_ref[0]
    for s in range(1, sources):
        total = total + parts_ref[s]
    stats = jnp.transpose(total[rows : rows + 8, :])
    mean = stats[:rows, 0:1] / width
    square = stats[:rows, 1:2] / width
    both = (total[:rows] - mean * total[rows + 2 : rows + 3]) * lax.rsqrt(square - mean * mean + EPS)
    swapped = pltpu.roll(both, lanes // 2, 1)
    first = lax.broadcasted_iota(jnp.int32, (rows, lanes), 1) < lanes // 2
    left_ref[...] = jnp.where(first, both, swapped)
    right = jnp.where(first, swapped, both)
    packed = jnp.where(first[: rows // 2], right[: rows // 2], right[rows // 2 :])
    for s in range(right_ref.shape[0]):
        right_ref[s] = packed


def pack_kernel(key_ref, value_ref, kv_ref):
    lanes = kv_ref.shape[2]
    tails = jnp.concatenate([key_ref[:, lanes:], value_ref[:, lanes:]], axis=1)
    packed = jnp.concatenate([key_ref[:, :lanes], value_ref[:, :lanes], tails], axis=0)
    for s in range(kv_ref.shape[0]):
        kv_ref[s] = packed


def bias_kernel(pair_ref, w_ref, out_ref):
    heads, steps, _ = out_ref.shape
    for r in range(steps):
        high, low = ksplit(channel_norm(pair_ref[r]))
        both = bdot(w_ref[...], jnp.concatenate([high, low], axis=1), ((1,), (1,)))
        out_ref[:, r, :] = both[:heads] + both[heads:]


def pair_bias(pair, w_bias):
    rows, cols, channels = pair.shape
    heads = w_bias.shape[1]
    high, low = split(w_bias.T)
    w = jnp.concatenate([jnp.concatenate([x, x], axis=1) for x in (high, low)], axis=0)
    block = pl.BlockSpec((BIAS_ROWS, cols, channels), lambda s: (s, 0, 0))
    return pl.pallas_call(
        bias_kernel,
        grid=(rows // BIAS_ROWS,),
        in_specs=[
            block,
            pl.BlockSpec(w.shape, lambda s: (0, 0)),
        ],
        out_specs=pl.BlockSpec((heads, BIAS_ROWS, cols), lambda s: (0, s, 0)),
        out_shape=jax.ShapeDtypeStruct((heads, rows, cols), F32),
        compiler_params=pltpu.CompilerParams(vmem_limit_bytes=24 * MIB),
        cost_estimate=pl.CostEstimate(
            flops=12 * rows * cols * channels * heads,
            bytes_accessed=4 * rows * cols * (channels + heads),
            transcendentals=rows * cols,
        ),
        name="pair_bias",
    )(pair, w)


def attention_kernel(place_ref, q_ref, own_ref, other_ref, bias_ref, out_ref):
    rows, lanes = q_ref.shape[1:]
    cols = bias_ref.shape[2]
    steps = out_ref.shape[0]
    group = bias_ref.shape[0] // steps
    hd = lanes // group
    even = place_ref[0] == 0
    scale = 1.0 / hd**0.5
    lane = lax.broadcasted_iota(jnp.int32, (rows, lanes), 1)
    for g in range(steps):
        heads = []
        for p in range(g * group // 2, (g + 1) * group // 2):
            own, other = own_ref[p], other_ref[p]
            heads += [jnp.where(even, own, other), jnp.where(even, other, own)]
        tails = jnp.concatenate([x[2 * hd :] for x in heads], axis=0)
        keys = jnp.concatenate([x[:hd] for x in heads], axis=0)
        keys = jnp.concatenate([keys, tails[:, : lanes // 2]], axis=1)
        values = jnp.concatenate([x[hd : 2 * hd] for x in heads], axis=0)
        values = jnp.concatenate([values, tails[:, lanes // 2 :]], axis=1)
        k_high, k_low = ksplit(keys)
        v_high, v_low = ksplit(values)
        q = q_ref[(pl.program_id(0) * steps + g) ^ place_ref[1]] * scale
        q = jnp.concatenate([jnp.where(lane // hd == h, q, 0.0) for h in range(group)], axis=0)
        q = jnp.concatenate(ksplit(q), axis=1)
        scores = bdot(q, jnp.concatenate([k_high, k_high], axis=0)) + bdot(q, jnp.concatenate([k_low, k_low], axis=0))
        scores = scores + bias_ref[g * group : (g + 1) * group].reshape(group * rows, cols)
        top = jnp.max(scores, axis=1, keepdims=True)
        expo = jnp.exp(scores - top)
        total = jnp.sum(expo, axis=1, keepdims=True)
        w = bdot(
            jnp.concatenate(ksplit(expo), axis=0), jnp.concatenate([v_high, v_low], axis=0), ((1,), (1,))
        )
        half = group * rows
        w = (w[:half, :lanes] + w[:half, lanes:]) + (w[half:, :lanes] + w[half:, lanes:])
        weighted = jnp.zeros((rows, lanes), F32)
        stats = jnp.zeros((rows, lanes), F32)
        for h in range(group):
            part = slice(h * rows, (h + 1) * rows)
            weighted = jnp.where(lane // hd == h, w[part], weighted)
            stats = jnp.where(lane == h, top[part], stats)
            stats = jnp.where(lane == h + group, total[part], stats)
        out_ref[g, :rows, :] = weighted
        stats = jnp.concatenate([stats, jnp.zeros((lanes - rows, lanes), F32)], axis=0)
        out_ref[g, rows:, :] = jnp.transpose(stats)[: 2 * group]


def attention(place, queries, own, other, bias):
    n_col, rows, lanes = queries.shape
    heads, _, cols = bias.shape
    group = heads // n_col
    steps = ATTENTION_GROUPS
    kv_block = pl.BlockSpec((steps * group // 2,) + own.shape[1:], lambda s: (s, 0, 0))
    return pl.pallas_call(
        attention_kernel,
        grid=(n_col // steps,),
        in_specs=[
            pl.BlockSpec(memory_space=pltpu.SMEM),
            pl.BlockSpec(queries.shape, lambda s: (0, 0, 0)),
            kv_block,
            kv_block,
            pl.BlockSpec((steps * group, rows, cols), lambda s: (s, 0, 0)),
        ],
        out_specs=pl.BlockSpec((steps, rows + 2 * group, lanes), lambda s: (s, 0, 0)),
        out_shape=jax.ShapeDtypeStruct((n_col, rows + 2 * group, lanes), F32),
        compiler_params=pltpu.CompilerParams(vmem_limit_bytes=24 * MIB),
        name="attention",
    )(place, queries, own, other, bias)


def update_kernel(
    place_ref, pair_ref, left_ref, own_ref, other_ref, w_diff_ref, bias_ref, w_prod_ref, w_up_ref, w_down_ref, out_ref,
    rights, base, diffs,
):
    step = pl.program_id(0)
    steps, _, lanes = pair_ref.shape

    @pl.when(step == 0)
    def _():
        w_diff = w_diff_ref[...]
        half = own_ref.shape[1]
        first = lax.broadcasted_iota(jnp.int32, (half, lanes), 1) < lanes // 2
        even = place_ref[0] == 0
        blocks = []
        for p in range(rights.shape[0] // (4 * half)):
            p = place_ref[1] * (rights.shape[0] // (4 * half)) + p
            own, other = own_ref[p], other_ref[p]
            blocks += [jnp.where(even, own, other), jnp.where(even, other, own)]
        for block, packed in enumerate(blocks):
            swapped = pltpu.roll(packed, lanes // 2, 1)
            start = 2 * half * block
            rights[start : start + half, :] = jnp.where(first, packed, swapped)
            rights[start + half : start + 2 * half, :] = jnp.where(first, swapped, packed)
        base[...] = bias_ref[...] - dot(rights[:, : lanes // 2], w_diff)
        diffs[...] = dot(left_ref[:, : lanes // 2], w_diff)

    first = lax.broadcasted_iota(jnp.int32, base.shape, 1) < lanes // 2

    def normalize(start):
        products, mid = [], []
        for r in range(start, start + CHUNK_ROWS):
            i = step * steps + r
            product = rights[...] * left_ref[pl.ds(i, 1), :]
            high = product.astype(BF).astype(F32)
            products.append(jnp.where(first, high, product - high).astype(BF))
            mid.append(pair_ref[r] + (base[...] + diffs[pl.ds(i, 1), :]))
        products = jnp.concatenate(products, axis=0)
        mid = jnp.concatenate(mid, axis=0) + bdot(jnp.concatenate([products, products], axis=1), w_prod_ref[...])
        high, low = ksplit(channel_norm(mid))
        return mid, jnp.concatenate([high, low, high, low], axis=1)

    def transition(start, mid, normed):
        hidden = ksplit(jnp.maximum(bdot(normed, w_up_ref[...]), 0.0))
        down = bdot(jnp.concatenate(hidden, axis=1), w_down_ref[...])
        out = mid + (down[:, :lanes] + down[:, lanes:])
        out_ref[start : start + CHUNK_ROWS] = out.reshape((CHUNK_ROWS,) + out_ref.shape[1:])

    current = normalize(0)
    for start in range(0, steps, CHUNK_ROWS):
        following = normalize(start + CHUNK_ROWS) if start + CHUNK_ROWS < steps else None
        transition(start, *current)
        current = following


def update_weights(w_outer, w_up, w_down):
    p_high, p_low = split(w_outer[: w_outer.shape[0] // 2])
    u_high, u_low = split(w_up)
    down = jnp.concatenate(split(w_down), axis=1)
    return (
        jnp.concatenate([p_high, p_high, p_low, p_low], axis=0),
        jnp.concatenate([u_high, u_high, u_low, u_low], axis=0),
        jnp.concatenate([down, down], axis=0),
    )


def update_pair(place, pair, left, rights, w_diff, outer_bias, w_prod, w_up, w_down):
    rows, cols, channels = pair.shape
    hidden = w_up.shape[1]
    whole = lambda x: pl.BlockSpec(x.shape, lambda s: (0,) * x.ndim)
    block = pl.BlockSpec((UPDATE_ROWS, cols, channels), lambda s: (s, 0, 0))
    fixed = (left, *rights, w_diff, outer_bias[None, :], w_prod, w_up, w_down)
    cells = rows * cols
    return pl.pallas_call(
        update_kernel,
        grid=(rows // UPDATE_ROWS,),
        in_specs=[pl.BlockSpec(memory_space=pltpu.SMEM), block] + [whole(x) for x in fixed],
        out_specs=block,
        out_shape=jax.ShapeDtypeStruct(pair.shape, F32),
        scratch_shapes=[
            pltpu.VMEM((cols, channels), F32),
            pltpu.VMEM((cols, channels), F32),
            pltpu.VMEM((rows, channels), F32),
        ],
        compiler_params=pltpu.CompilerParams(vmem_limit_bytes=50 * MIB),
        cost_estimate=pl.CostEstimate(
            flops=2 * cells * channels * (8 * hidden + 256),
            bytes_accessed=8 * cells * channels,
            transcendentals=cells,
        ),
        name="update_pair",
    )(place, pair, *fixed)


def after(x, *others):
    place = pl.BlockSpec(memory_space=pl.ANY)
    return pl.pallas_call(
        lambda *refs: None,
        in_specs=[place] * (1 + len(others)),
        out_specs=place,
        out_shape=jax.ShapeDtypeStruct(x.shape, x.dtype),
        input_output_aliases={0: 0},
        compiler_params=pltpu.CompilerParams(vmem_limit_bytes=MIB),
        name="after",
    )(x, *others)


def per_device(
    seq, query, key, value, pair, w_bias, w_out, w_left, w_right, w_outer, outer_bias, w_up, w_down
):
    rows, cols, channels = pair.shape
    heads = w_bias.shape[1]
    width = w_out.shape[0]
    head_dim = width // heads
    n_row, n_col = lax.axis_size("row"), lax.axis_size("col")
    group = heads // n_col

    kv = pl.pallas_call(
        pack_kernel,
        out_shape=jax.ShapeDtypeStruct((n_row // 2, 3 * head_dim, channels), F32),
        name="pack",
    )(key.T, value.T)
    queries = query[None]
    hop = 1
    while hop < n_col:
        other = lax.ppermute(queries, "col", [(i, i ^ hop) for i in range(n_col)])
        queries = jnp.concatenate([queries, other], axis=0)
        hop *= 2
    pairs = [[z * 2 + k for z in range(n_row // 2)] for k in range(2)]
    own = lax.all_to_all(kv, "row", 0, 0, axis_index_groups=pairs)
    bias = pair_bias(pair, w_bias)
    weights = update_weights(w_outer, w_up, w_down)
    w_out = jnp.concatenate(split(w_out), axis=1)
    w_lr = jnp.concatenate([w_left, w_right], axis=1)
    own = after(own, queries, bias, w_out, w_lr, *weights)
    across = [(i, i ^ 1) for i in range(n_row)]
    other = lax.ppermute(own, "row", across)
    place = jnp.stack([lax.axis_index("row") % 2, lax.axis_index("col")])
    parts = attention(place, queries, own, other, bias)
    parts = lax.all_to_all(parts, "col", 0, 0)

    attn = pl.pallas_call(
        functools.partial(merge_kernel, group),
        out_shape=jax.ShapeDtypeStruct((n_col, rows, channels), F32),
        compiler_params=pltpu.CompilerParams(vmem_limit_bytes=8 * MIB),
        name="merge",
    )(parts)
    attn = lax.all_to_all(attn, "col", 0, 0)
    seq_new, shares = pl.pallas_call(
        project_kernel,
        out_shape=(
            jax.ShapeDtypeStruct(seq.shape, F32),
            jax.ShapeDtypeStruct((n_col, rows + 8, channels), F32),
        ),
        compiler_params=pltpu.CompilerParams(vmem_limit_bytes=8 * MIB),
        name="project",
    )(attn, w_out, seq, w_lr)
    shares = lax.all_to_all(shares, "col", 0, 0)
    left, right = pl.pallas_call(
        functools.partial(left_right_kernel, width),
        out_shape=(
            jax.ShapeDtypeStruct((rows, channels), F32),
            jax.ShapeDtypeStruct((n_row // 2, rows // 2, channels), F32),
        ),
        compiler_params=pltpu.CompilerParams(vmem_limit_bytes=8 * MIB),
        name="left_right",
    )(shares)
    right = lax.all_to_all(right, "row", 0, 0, axis_index_groups=pairs)
    rights = (right, lax.ppermute(right, "row", across))
    return seq_new, update_pair(place, pair, left, rights, w_outer[w_outer.shape[0] // 2 :], outer_bias, *weights)


def solution(mesh):
    in_specs = (
        P("row", "col"),
        P("row", "col"),
        P("col", "row"),
        P("col", "row"),
        P("row", "col", None),
        P(),
        P(None, "col"),
        P("col", None),
        P("col", None),
        P(),
        P(),
        P(),
        P(),
    )
    out_specs = (P("row", "col"), P("row", "col", None))
    return jax.shard_map(
        per_device, mesh=mesh, in_specs=in_specs, out_specs=out_specs, check_vma=False
    )
```

time: 171 us -> 117 us (0.68)
  blocking collectives: 11.7 us -> 44.4 us
  waiting for transfers between devices: 37.5 us -> 6.77 us
  matrix products: 16.3 us -> 0 us
  local copies, waits for them, and re-layouts: 20.4 us -> 6.98 us
  Pallas kernels: 36.5 us -> 26.9 us
  starting transfers between devices: 33.3 us -> 25.3 us
  other arithmetic: 13.2 us -> 5.56 us
    all_to_all x5 -> x1, waiting for transfers between devices: 37.5 us -> 1.22 us  [per_device(): own = lax.all_to_all(kv, 'row', 0, 0, axis_index_groups=pairs)]
    all_to_all x1 -> x4, blocking collectives: 11.7 us -> 44.4 us  [the longest x1 17.6 us: per_device(): right = lax.all_to_all(right, 'row', 0, 0, axis_index_groups=pairs)]
    all_to_all x5 -> x1, starting transfers between devices: 30 us -> 10.6 us  [per_device(): own = lax.all_to_all(kv, 'row', 0, 0, axis_index_groups=pairs)]
    dot_general x3 -> x0, matrix products: 16.3 us -> none  [the longest x1 12.2 us: per_device(): bias = jnp.einsum('ijc,ch->hij', channel_norm(pair), w_bias, precision=HIGH)]
    ppermute x1 -> x5, starting transfers between devices: 3.37 us -> 14.6 us  [the longest x3 6.05 us: per_device(): other = lax.ppermute(queries, 'col', [(i, i ^ hop) for i in range(n_col)])]
    reduce_sum x3 -> x0, other arithmetic: 9.5 us -> none  [the longest x1 4.94 us: channel_norm(): jnp.mean(centre * centre, axis=-1, keepdims=True) + EPS]
    slice x5 -> x0, local copies, waits for them, and re-layouts: 7.18 us -> none  [the longest x2 4.27 us: per_device(): values = kv[1].reshape(heads, cols, head_dim)]
    ppermute x1 -> x5, waiting for transfers between devices: 0.01 us -> 5.55 us  [the longest x3 2.52 us: per_device(): other = lax.ppermute(queries, 'col', [(i, i ^ hop) for i in range(n_col)])]
  transfers between devices with their start and end apart: 6 -> 6, of which waited for: 4 -> 4; matrix products, arithmetic and copies ran while one was open for 14% -> 6% of each run, Pallas kernels for 0% -> 6%
where the time goes in v2:
time: 117 us
  blocking collectives  44.4 us (38%)
  Pallas kernels  26.9 us (23%)
  starting transfers between devices  25.3 us (22%)
  local copies, waits for them, and re-layouts  6.98 us (6%)
  waiting for transfers between devices  6.77 us (6%)
  other arithmetic  5.56 us (5%)
    all_to_all x1, blocking collectives, per_device(): right = lax.all_to_all(right, 'row', 0, 0, axis_index_groups=pairs)  17.6 us
    pallas_call x1, Pallas kernels, update_pair(): pl.pallas_call(update_kernel, grid=(rows // UPDATE_ROWS,), in_specs=[pl.B...  16.1 us
    all_to_all x1, starting transfers between devices, per_device(): own = lax.all_to_all(kv, 'row', 0, 0, axis_index_groups=pairs)  10.6 us
    all_to_all x1, blocking collectives, per_device(): parts = lax.all_to_all(parts, 'col', 0, 0)  9.76 us
    all_to_all x1, blocking collectives, per_device(): attn = lax.all_to_all(attn, 'col', 0, 0)  8.51 us
    all_to_all x1, blocking collectives, per_device(): shares = lax.all_to_all(shares, 'col', 0, 0)  8.45 us
    unnamed x30, local copies, waits for them, and re-layouts  6.98 us
    ppermute x3, starting transfers between devices, per_device(): other = lax.ppermute(queries, 'col', [(i, i ^ hop) for i in range(n_col)])  6.05 us
  transfers between devices with their start and end apart: 6, of which 4 were waited for; matrix products, arithmetic and copies ran while one was open for 6% of the time, Pallas kernels for 6%

profile of v2, /device:TPU:1, one launch (start us, length us, event | category | flops | bytes accessed | tf_op | source)
XLA Modules:
  0.0 116.7 jit_solution(9347035922671541371)
XLA Ops:
  0.6 0.0 copy-start.8
  0.6 0.0 copy-start.13
  0.7 0.0 copy-start.12
  0.7 2.2 %collective-permute-start = (f32[1,48,128]{2,1,0:T(8,128)}, f32[1,48,128]{2,1,0:T(8,128)S(1)}, u32[]{:S(2)}, u32[]{:S(2)}) collective-permute-start(f32[1,48,128]{2,1,0:T(8,128)} %bitcast.10), channel_id=1, source_target_pairs={{0,1},{1,0},{2,3},{3,2},{4,5},{5,4},{6,7},{7,6},{8,9},{9,8},{10,11... | collective-permute-start | bytes 73736 | tf_op jit(solution)/shard_map/ppermute | solution.py:340
  2.9 1.7 %pack.1 = f32[16,96,128]{2,1,0:T(8,128)} custom-call(f32[32,192]{1,0:T(8,128)} %bitcast.14, f32[32,192]{1,0:T(8,128)} %bitcast.15), custom_call_target="tpu_custom_call" | custom-call | tf_op jit(solution)/shard_map/pack/pallas_call | solution.py:332
  4.6 10.6 %all-to-all-start = ((f32[16,96,128]{2,1,0:T(8,128)}), f32[16,96,128]{2,1,0:T(8,128)S(1)}, u32[]{:S(2)}, u32[]{:S(2)}) async-start(f32[16,96,128]{2,1,0:T(8,128)} %pack.1), calls=%async_computation | async-start | bytes 1572864 | tf_op jit(solution)/shard_map/all_to_all | solution.py:344
  15.3 1.0 reduce-precision_convert_fusion.2
  16.2 1.1 reduce-precision_convert_fusion
  17.4 1.0 reduce-precision_convert_fusion.1
  18.4 0.8 copy.16
  19.2 0.9 copy.17
  20.1 0.0 copy-start.9
  20.1 0.9 pad_maximum_fusion.1.refs_6_.w_up_ref
  21.0 0.1 pad_maximum_fusion
  21.1 0.0 copy-done.13
  21.1 0.0 copy-done.12
  21.1 0.6 fusion.5
  21.7 0.1 pad_maximum_fusion.4.refs_4_.w_lr_ref
  21.8 0.0 collective-permute-done
  21.8 0.0 copy-done.8
  21.8 0.0 copy-start.10
  21.8 1.3 %collective-permute-start.1 = (f32[2,48,128]{2,1,0:T(8,128)S(1)}, f32[2,48,128]{2,1,0:T(8,128)S(1)}, u32[]{:S(2)}, u32[]{:S(2)}) collective-permute-start(f32[2,48,128]{2,1,0:T(8,128)S(1)} %pad_maximum_fusion.6), channel_id=1, source_target_pairs={{0,2},{1,3},{2,0},{3,1},{4,6},{5,7},{6,4},{7,5},{8,10},{9,11},{10,... | collective-permute-start | bytes 147464 | tf_op jit(solution)/shard_map/ppermute | solution.py:340
  23.1 0.0 copy-done.10
  23.2 2.3 %copy-done = f32[48,192,128]{2,1,0:T(8,128)S(1)} copy-done((f32[48,192,128]{2,1,0:T(8,128)S(1)}, f32[48,192,128]{2,1,0:T(8,128)}, u32[]{:S(2)}) %copy-start) | copy-done | bytes 4718616
  25.5 4.7 %pair_bias.1.refs_2_.bias_ref = f32[32,48,192]{2,1,0:T(8,128)S(1)} custom-call(f32[48,192,128]{2,1,0:T(8,128)S(1)} %copy-done, bf16[64,256]{1,0:T(8,128)(2,1)S(1)} %maximum_maximum_fusion.1.w_ref), custom_call_target="tpu_custom_call" | custom-call | flops 452984832 | bytes 5898240 | tf_op jit(solution)/shard_map/pair_bias/pallas_call | solution.py:128
  30.2 0.0 collective-permute-done.1
  30.2 0.0 copy-done.9
  30.2 2.5 %collective-permute-start.2 = (f32[4,48,128]{2,1,0:T(8,128)S(1)}, f32[4,48,128]{2,1,0:T(8,128)S(1)}, u32[]{:S(2)}, u32[]{:S(2)}) collective-permute-start(f32[4,48,128]{2,1,0:T(8,128)S(1)} %pad_maximum_fusion.3), channel_id=1, source_target_pairs={{0,4},{1,5},{2,6},{3,7},{4,0},{5,1},{6,2},{7,3},{8,12},{9,13},{10,... | collective-permute-start | bytes 294920 | tf_op jit(solution)/shard_map/ppermute | solution.py:340
  32.8 2.5 %collective-permute-done.2 = f32[4,48,128]{2,1,0:T(8,128)S(1)} collective-permute-done((f32[4,48,128]{2,1,0:T(8,128)S(1)}, f32[4,48,128]{2,1,0:T(8,128)S(1)}, u32[]{:S(2)}, u32[]{:S(2)}) %collective-permute-start.2) | collective-permute-done | bytes 98336 | tf_op jit(solution)/shard_map/ppermute | solution.py:340
  35.3 0.7 pad_maximum_fusion.2.refs_1_.q_ref
  36.0 1.2 %all-to-all-done.refs_0_ = f32[16,96,128]{2,1,0:T(8,128)S(1)} async-done(((f32[16,96,128]{2,1,0:T(8,128)}), f32[16,96,128]{2,1,0:T(8,128)S(1)}, u32[]{:S(2)}, u32[]{:S(2)}) %all-to-all-start) | async-done | bytes 786464 | tf_op jit(solution)/shard_map/all_to_all | solution.py:344
  37.2 1.0 copy-done.1
  38.2 0.9 copy-done.3
  39.2 3.4 %collective-permute-start.3 = (f32[16,96,128]{2,1,0:T(8,128)S(1)}, f32[16,96,128]{2,1,0:T(8,128)}, u32[]{:S(2)}, u32[]{:S(2)}) collective-permute-start(f32[16,96,128]{2,1,0:T(8,128)S(1)} %after.1.own_ref), channel_id=1, source_target_pairs={{0,8},{8,0},{16,24},{24,16},{32,40},{40,32},{48,56},{56,48},{64,72... | collective-permute-start | bytes 2359304 | tf_op jit(solution)/shard_map/ppermute | solution.py:351
  42.6 0.1 pad_add_fusion.place_ref
  42.7 2.0 %collective-permute-done.3.other_ref = f32[16,96,128]{2,1,0:T(8,128)} collective-permute-done((f32[16,96,128]{2,1,0:T(8,128)S(1)}, f32[16,96,128]{2,1,0:T(8,128)}, u32[]{:S(2)}, u32[]{:S(2)}) %collective-permute-start.3) | collective-permute-done | bytes 786464 | tf_op jit(solution)/shard_map/ppermute | solution.py:351
  44.6 0.9 copy-done.4
  45.6 2.8 %attention.1 = f32[8,56,128]{2,1,0:T(8,128)S(1)} custom-call(s32[2]{0:T(128)S(1)} %pad_add_fusion.place_ref, f32[8,48,128]{2,1,0:T(8,128)S(1)} %copy-done.4, f32[16,96,128]{2,1,0:T(8,128)S(1)} %after.1.own_ref, f32[16,96,128]{2,1,0:T(8,128)} %collective-permute-done.3.other_ref, f32[32,48,192]{2,1,0:T(8,128)S(1)} %pair_bias.1.refs_2_.bias_ref), custom_call_target="tpu_custom_call" | custom-call | tf_op jit(solution)/shard_map/attention/pallas_call | solution.py:199
  48.3 9.8 %all_to_all.25.parts_ref = f32[8,56,128]{2,1,0:T(8,128)S(1)} all-to-all(f32[8,56,128]{2,1,0:T(8,128)S(1)} %attention.1), channel_id=1, replica_groups=mesh['row'=32,'col'=8] {'col'}, dimensions={0} | all-to-all | bytes 458752 | tf_op jit(solution)/shard_map/all_to_all | solution.py:354
  58.1 0.4 merge.1
  58.6 8.5 %all_to_all.26.attn_ref = f32[8,48,128]{2,1,0:T(8,128)S(1)} all-to-all(f32[8,48,128]{2,1,0:T(8,128)S(1)} %merge.1), channel_id=1, replica_groups=mesh['row'=32,'col'=8] {'col'}, dimensions={0} | all-to-all | bytes 393216 | tf_op jit(solution)/shard_map/all_to_all | solution.py:362
  67.1 0.9 project.1
  68.0 8.5 %all_to_all.27.parts_ref = f32[8,56,128]{2,1,0:T(8,128)S(1)} all-to-all(f32[8,56,128]{2,1,0:T(8,128)S(1)} %get-tuple-element.7), channel_id=1, replica_groups=mesh['row'=32,'col'=8] {'col'}, dimensions={0} | all-to-all | bytes 458752 | tf_op jit(solution)/shard_map/all_to_all | solution.py:372
  76.4 0.3 left_right.1
  76.7 17.6 %all_to_all.28.own_ref = f32[16,24,128]{2,1,0:T(8,128)S(1)} all-to-all(f32[16,24,128]{2,1,0:T(8,128)S(1)} %get-tuple-element.9), channel_id=1, replica_groups={{0,16,32,48,64,80,96,112,128,144,160,176,192,208,224,240},{8,24,40,56,7..., dimensions={0} | all-to-all | bytes 393216 | tf_op jit(solution)/shard_map/all_to_all | solution.py:382
  94.3 5.2 %collective-permute-start.4 = (f32[16,24,128]{2,1,0:T(8,128)S(1)}, f32[16,24,128]{2,1,0:T(8,128)S(1)}, u32[]{:S(2)}, u32[]{:S(2)}) collective-permute-start(f32[16,24,128]{2,1,0:T(8,128)S(1)} %all_to_all.28.own_ref), channel_id=1, source_target_pairs={{0,8},{8,0},{16,24},{24,16},{32,40},{40,32},{48,56},{56,48},{64,72... | collective-permute-start | bytes 589832 | tf_op jit(solution)/shard_map/ppermute | solution.py:383
  99.5 1.1 collective-permute-done.4.other_ref
  100.6 16.1 %update_pair.1 = f32[48,192,128]{2,1,0:T(8,128)} custom-call(s32[2]{0:T(128)S(1)} %pad_add_fusion.place_ref, f32[48,192,128]{2,1,0:T(8,128)} %pair_ref.3, f32[48,128]{1,0:T(8,128)S(1)} %get-tuple-element.8.left_ref, f32[16,24,128]{2,1,0:T(8,128)S(1)} %all_to_all.28.own_ref, f32[16,24,128]{2,1,0:T(8,128)S(1)} %collective-permute-done.4.other_ref, ...), custom_call_target="tpu_custom_call" | custom-call | flops 10267656192 | bytes 9437184 | tf_op jit(solution)/shard_map/update_pair/pallas_call | solution.py:288
  (20 shorter events, 0.1 us)
Async XLA Ops:
  0.6 21.2 %copy-start.8 = (f32[48,128]{1,0:T(8,128)S(1)}, f32[48,128]{1,0:T(8,128)}, u32[]{:S(2)}) copy-start(f32[48,128]{1,0:T(8,128)} %param.14) | copy-start | bytes 73732
  0.6 20.4 %copy-start.13 = (f32[128,32]{0,1:T(8,128)S(1)}, f32[128,32]{0,1:T(8,128)}, u32[]{:S(2)}) copy-start(f32[128,32]{0,1:T(8,128)} %param.18) | copy-start | bytes 49156
  0.7 20.4 %copy-start.12 = (f32[128,128]{1,0:T(8,128)S(1)}, f32[128,128]{1,0:T(8,128)}, u32[]{:S(2)}) copy-start(f32[128,128]{1,0:T(8,128)} %param.22) | copy-start | bytes 196612
  0.7 21.1 %collective-permute-start = (f32[1,48,128]{2,1,0:T(8,128)}, f32[1,48,128]{2,1,0:T(8,128)S(1)}, u32[]{:S(2)}, u32[]{:S(2)}) collective-permute-start(f32[1,48,128]{2,1,0:T(8,128)} %bitcast.10), channel_id=1, source_target_pairs={{0,1},{1,0},{2,3},{3,2},{4,5},{5,4},{6,7},{7,6},{8,9},{9,8},{10,11... | collective-permute-start | bytes 73736 | tf_op jit(solution)/shard_map/ppermute | solution.py:340
  4.6 32.6 %all-to-all-start = ((f32[16,96,128]{2,1,0:T(8,128)}), f32[16,96,128]{2,1,0:T(8,128)S(1)}, u32[]{:S(2)}, u32[]{:S(2)}) async-start(f32[16,96,128]{2,1,0:T(8,128)} %pack.1), calls=%async_computation | async-start | bytes 1572864 | tf_op jit(solution)/shard_map/all_to_all | solution.py:344
  20.1 10.1 %copy-start.9 = (f32[48,128]{1,0:T(8,128)S(1)}, f32[48,128]{1,0:T(8,128)}, u32[]{:S(2)}) copy-start(f32[48,128]{1,0:T(8,128)} %param.14) | copy-start | bytes 73732
  21.8 1.3 %copy-start.10 = (f32[1,48,128]{2,1,0:T(8,128)}, f32[1,48,128]{2,1,0:T(8,128)S(1)}, u32[]{:S(2)}) copy-start(f32[1,48,128]{2,1,0:T(8,128)S(1)} %collective-permute-done) | copy-start | bytes 73732
  21.8 8.3 %collective-permute-start.1 = (f32[2,48,128]{2,1,0:T(8,128)S(1)}, f32[2,48,128]{2,1,0:T(8,128)S(1)}, u32[]{:S(2)}, u32[]{:S(2)}) collective-permute-start(f32[2,48,128]{2,1,0:T(8,128)S(1)} %pad_maximum_fusion.6), channel_id=1, source_target_pairs={{0,2},{1,3},{2,0},{3,1},{4,6},{5,7},{6,4},{7,5},{8,10},{9,11},{10,... | collective-permute-start | bytes 147464 | tf_op jit(solution)/shard_map/ppermute | solution.py:340
  23.2 2.3 %copy-start = (f32[48,192,128]{2,1,0:T(8,128)S(1)}, f32[48,192,128]{2,1,0:T(8,128)}, u32[]{:S(2)}) copy-start(f32[48,192,128]{2,1,0:T(8,128)} %pair_ref.3) | copy-start | bytes 14155780
  25.5 4.7 %copy-start.11 = (f32[1,48,128]{2,1,0:T(8,128)S(1)}, f32[1,48,128]{2,1,0:T(8,128)}, u32[]{:S(2)}) copy-start(f32[1,48,128]{2,1,0:T(8,128)} %copy-done.10) | copy-start | bytes 73732
  30.2 5.1 %collective-permute-start.2 = (f32[4,48,128]{2,1,0:T(8,128)S(1)}, f32[4,48,128]{2,1,0:T(8,128)S(1)}, u32[]{:S(2)}, u32[]{:S(2)}) collective-permute-start(f32[4,48,128]{2,1,0:T(8,128)S(1)} %pad_maximum_fusion.3), channel_id=1, source_target_pairs={{0,4},{1,5},{2,6},{3,7},{4,0},{5,1},{6,2},{7,3},{8,12},{9,13},{10,... | collective-permute-start | bytes 294920 | tf_op jit(solution)/shard_map/ppermute | solution.py:340
  37.2 1.0 copy-start.1
  38.2 0.9 copy-start.3
  39.2 61.4 %copy-start.7 = (f32[128]{0:T(128)S(1)}, f32[128]{0:T(128)}, u32[]{:S(2)}) copy-start(f32[128]{0:T(128)} %param.23) | copy-start | bytes 1540
  39.2 5.5 %collective-permute-start.3 = (f32[16,96,128]{2,1,0:T(8,128)S(1)}, f32[16,96,128]{2,1,0:T(8,128)}, u32[]{:S(2)}, u32[]{:S(2)}) collective-permute-start(f32[16,96,128]{2,1,0:T(8,128)S(1)} %after.1.own_ref), channel_id=1, source_target_pairs={{0,8},{8,0},{16,24},{24,16},{32,40},{40,32},{48,56},{56,48},{64,72... | collective-permute-start | bytes 2359304 | tf_op jit(solution)/shard_map/ppermute | solution.py:351
  42.6 58.0 %copy-start.2 = (bf16[512,512]{1,0:T(8,128)(2,1)S(1)}, bf16[512,512]{1,0:T(8,128)(2,1)}, u32[]{:S(2)}) copy-start(bf16[512,512]{1,0:T(8,128)(2,1)} %pad_maximum_fusion.1.refs_6_.w_up_ref) | copy-start | bytes 1572868
  44.6 0.9 copy-start.4
  45.6 21.5 %copy-start.6 = (f32[48,128]{1,0:T(8,128)S(1)}, f32[48,128]{1,0:T(8,128)}, u32[]{:S(2)}) copy-start(f32[48,128]{1,0:T(8,128)} %seq_ref.1) | copy-start | bytes 73732
  45.6 55.0 %copy-start.5 = (f32[64,128]{1,0:T(8,128)S(1)}, f32[64,128]{1,0:T(8,128)}, u32[]{:S(2)}) copy-start(f32[64,128]{1,0:T(8,128)} %get-tuple-element.16.w_diff_ref) | copy-start | bytes 98308
  94.3 6.2 %collective-permute-start.4 = (f32[16,24,128]{2,1,0:T(8,128)S(1)}, f32[16,24,128]{2,1,0:T(8,128)S(1)}, u32[]{:S(2)}, u32[]{:S(2)}) collective-permute-start(f32[16,24,128]{2,1,0:T(8,128)S(1)} %all_to_all.28.own_ref), channel_id=1, source_target_pairs={{0,8},{8,0},{16,24},{24,16},{32,40},{40,32},{48,56},{56,48},{64,72... | collective-permute-start | bytes 589832 | tf_op jit(solution)/shard_map/ppermute | solution.py:383

commit v3 on v2

--- a/solution.py
+++ b/solution.py
@@ -12,10 +12,13 @@
 BF = jnp.bfloat16
 F32 = jnp.float32
 BIAS_ROWS = 16
-ATTENTION_GROUPS = 4
 UPDATE_ROWS = 24
 CHUNK_ROWS = 4
 MIB = 2**20
+HOPS = (
+    ((2, 1), (3, 1), (3, 0), (0, 1), (0, 0), (1, 0), (1, 1), (2, 0)),
+    ((2, 0), (1, 0), (3, 1), (0, 0), (0, 1), (1, 1), (2, 1), (3, 0)),
+)
 
 
 def dot(a, b, dims=((1,), (0,)), precision=HIGH):
@@ -29,11 +32,6 @@
 def channel_norm(x):
     centre = x - jnp.mean(x, axis=-1, keepdims=True)
     return centre * lax.rsqrt(jnp.mean(centre * centre, axis=-1, keepdims=True) + EPS)
-
-
-def split(x):
-    high = lax.reduce_precision(x, 8, 7)
-    return high.astype(BF), (x - high).astype(BF)
 
 
 def ksplit(x):
@@ -62,21 +60,21 @@
         out_ref[s] = attn
 
 
-def project_kernel(attn_ref, w_out_ref, seq_ref, w_lr_ref, seq_new_ref, out_ref):
+def project_kernel(attn_ref, w_out_ref, seq_ref, w_left_ref, w_right_ref, seq_new_ref, out_ref):
     sources, rows, lanes = attn_ref.shape
     attn = jnp.concatenate([attn_ref[s] for s in range(sources)], axis=1)
-    both = bdot(jnp.concatenate(ksplit(attn), axis=0), w_out_ref[...])
+    both = bdot(jnp.concatenate(ksplit(attn), axis=0), jnp.concatenate(ksplit(w_out_ref[...]), axis=1))
     both = both[:, :lanes] + both[:, lanes:]
     total = seq_ref[...] + (both[:rows] + both[rows:])
     seq_new_ref[...] = total
-    w_lr = w_lr_ref[...]
-    part = dot(total, w_lr)
+    w_lr = jnp.concatenate([w_left_ref[...], w_right_ref[...]], axis=0)
+    part = dot(total, w_lr, ((1,), (1,)))
     ones = jnp.ones((8, lanes), F32)
     sums = dot(ones, total, ((1,), (1,)))
     squares = dot(ones, total * total, ((1,), (1,)))
     row = lax.broadcasted_iota(jnp.int32, (8, rows), 0)
     stats = jnp.where(row == 0, sums, squares)
-    columns = jnp.sum(w_lr, axis=0, keepdims=True)
+    columns = dot(ones, w_lr, ((1,), (1,)))[:1]
     for s in range(out_ref.shape[0]):
         out_ref[s, :rows, :] = part
         out_ref[s, rows : rows + 8, :] = jnp.zeros((8, lanes), F32)
@@ -98,9 +96,7 @@
     first = lax.broadcasted_iota(jnp.int32, (rows, lanes), 1) < lanes // 2
     left_ref[...] = jnp.where(first, both, swapped)
     right = jnp.where(first, swapped, both)
-    packed = jnp.where(first[: rows // 2], right[: rows // 2], right[rows // 2 :])
-    for s in range(right_ref.shape[0]):
-        right_ref[s] = packed
+    right_ref[...] = jnp.where(first[: rows // 2], right[: rows // 2], right[rows // 2 :])
 
 
 def pack_kernel(key_ref, value_ref, kv_ref):
@@ -111,19 +107,20 @@
         kv_ref[s] = packed
 
 
-def bias_kernel(pair_ref, w_ref, out_ref):
+def bias_kernel(pair_ref, w_ref, out_ref, done_ref):
     heads, steps, _ = out_ref.shape
+    done_ref[...] = jnp.zeros(done_ref.shape, F32)
+    w = jnp.concatenate([jnp.concatenate([x, x], axis=1) for x in ksplit(w_ref[...])], axis=0)
     for r in range(steps):
         high, low = ksplit(channel_norm(pair_ref[r]))
-        both = bdot(w_ref[...], jnp.concatenate([high, low], axis=1), ((1,), (1,)))
+        both = bdot(w, jnp.concatenate([high, low], axis=1), ((1,), (1,)))
         out_ref[:, r, :] = both[:heads] + both[heads:]
 
 
 def pair_bias(pair, w_bias):
     rows, cols, channels = pair.shape
     heads = w_bias.shape[1]
-    high, low = split(w_bias.T)
-    w = jnp.concatenate([jnp.concatenate([x, x], axis=1) for x in (high, low)], axis=0)
+    w = w_bias.T
     block = pl.BlockSpec((BIAS_ROWS, cols, channels), lambda s: (s, 0, 0))
     return pl.pallas_call(
         bias_kernel,
@@ -132,8 +129,11 @@
             block,
             pl.BlockSpec(w.shape, lambda s: (0, 0)),
         ],
-        out_specs=pl.BlockSpec((heads, BIAS_ROWS, cols), lambda s: (0, s, 0)),
-        out_shape=jax.ShapeDtypeStruct((heads, rows, cols), F32),
+        out_specs=(
+            pl.BlockSpec((heads, BIAS_ROWS, cols), lambda s: (0, s, 0)),
+            pl.BlockSpec((8, 128), lambda s: (0, 0)),
+        ),
+        out_shape=(jax.ShapeDtypeStruct((heads, rows, cols), F32), jax.ShapeDtypeStruct((8, 128), F32)),
         compiler_params=pltpu.CompilerParams(vmem_limit_bytes=24 * MIB),
         cost_estimate=pl.CostEstimate(
             flops=12 * rows * cols * channels * heads,
@@ -144,7 +144,7 @@
     )(pair, w)
 
 
-def attention_kernel(place_ref, q_ref, own_ref, other_ref, bias_ref, out_ref):
+def attention_kernel(place_ref, q_ref, far_ref, own_ref, other_ref, bias_ref, out_ref):
     rows, lanes = q_ref.shape[1:]
     cols = bias_ref.shape[2]
     steps = out_ref.shape[0]
@@ -165,7 +165,10 @@
         values = jnp.concatenate([values, tails[:, lanes // 2 :]], axis=1)
         k_high, k_low = ksplit(keys)
         v_high, v_low = ksplit(values)
-        q = q_ref[(pl.program_id(0) * steps + g) ^ place_ref[1]] * scale
+        slot = g ^ place_ref[1]
+        near = slot < q_ref.shape[0]
+        slot = lax.rem(slot, q_ref.shape[0])
+        q = jnp.where(near, q_ref[slot], far_ref[slot]) * scale
         q = jnp.concatenate([jnp.where(lane // hd == h, q, 0.0) for h in range(group)], axis=0)
         q = jnp.concatenate(ksplit(q), axis=1)
         scores = bdot(q, jnp.concatenate([k_high, k_high], axis=0)) + bdot(q, jnp.concatenate([k_low, k_low], axis=0))
@@ -190,45 +193,34 @@
         out_ref[g, rows:, :] = jnp.transpose(stats)[: 2 * group]
 
 
-def attention(place, queries, own, other, bias):
-    n_col, rows, lanes = queries.shape
+def attention(place, queries, far_queries, own, other, bias):
+    n_col, rows, lanes = 2 * queries.shape[0], *queries.shape[1:]
     heads, _, cols = bias.shape
     group = heads // n_col
-    steps = ATTENTION_GROUPS
-    kv_block = pl.BlockSpec((steps * group // 2,) + own.shape[1:], lambda s: (s, 0, 0))
     return pl.pallas_call(
         attention_kernel,
-        grid=(n_col // steps,),
-        in_specs=[
-            pl.BlockSpec(memory_space=pltpu.SMEM),
-            pl.BlockSpec(queries.shape, lambda s: (0, 0, 0)),
-            kv_block,
-            kv_block,
-            pl.BlockSpec((steps * group, rows, cols), lambda s: (s, 0, 0)),
-        ],
-        out_specs=pl.BlockSpec((steps, rows + 2 * group, lanes), lambda s: (s, 0, 0)),
+        in_specs=[pl.BlockSpec(memory_space=pltpu.SMEM)] + [pl.BlockSpec(memory_space=pltpu.VMEM)] * 5,
         out_shape=jax.ShapeDtypeStruct((n_col, rows + 2 * group, lanes), F32),
         compiler_params=pltpu.CompilerParams(vmem_limit_bytes=24 * MIB),
         name="attention",
-    )(place, queries, own, other, bias)
+    )(place, queries, far_queries, own, other, bias)
 
 
 def update_kernel(
-    place_ref, pair_ref, left_ref, own_ref, other_ref, w_diff_ref, bias_ref, w_prod_ref, w_up_ref, w_down_ref, out_ref,
-    rights, base, diffs,
+    place_ref, pair_ref, left_ref, own_ref, other_ref, w_outer_ref, bias_ref, w_up_ref, w_down_ref, out_ref,
+    rights, base, diffs, w_prod, w_ups, w_downs,
 ):
     step = pl.program_id(0)
     steps, _, lanes = pair_ref.shape
 
     @pl.when(step == 0)
     def _():
-        w_diff = w_diff_ref[...]
+        w_diff = w_outer_ref[lanes // 2 :, :]
         half = own_ref.shape[1]
         first = lax.broadcasted_iota(jnp.int32, (half, lanes), 1) < lanes // 2
         even = place_ref[0] == 0
         blocks = []
         for p in range(rights.shape[0] // (4 * half)):
-            p = place_ref[1] * (rights.shape[0] // (4 * half)) + p
             own, other = own_ref[p], other_ref[p]
             blocks += [jnp.where(even, own, other), jnp.where(even, other, own)]
         for block, packed in enumerate(blocks):
@@ -238,6 +230,12 @@
             rights[start + half : start + 2 * half, :] = jnp.where(first, swapped, packed)
         base[...] = bias_ref[...] - dot(rights[:, : lanes // 2], w_diff)
         diffs[...] = dot(left_ref[:, : lanes // 2], w_diff)
+        high, low = ksplit(w_outer_ref[: lanes // 2, :])
+        w_prod[...] = jnp.concatenate([high, high, low, low], axis=0)
+        high, low = ksplit(w_up_ref[...])
+        w_ups[...] = jnp.concatenate([high, high, low, low], axis=0)
+        both = jnp.concatenate(ksplit(w_down_ref[...]), axis=1)
+        w_downs[...] = jnp.concatenate([both, both], axis=0)
 
     first = lax.broadcasted_iota(jnp.int32, base.shape, 1) < lanes // 2
 
@@ -250,13 +248,13 @@
             products.append(jnp.where(first, high, product - high).astype(BF))
             mid.append(pair_ref[r] + (base[...] + diffs[pl.ds(i, 1), :]))
         products = jnp.concatenate(products, axis=0)
-        mid = jnp.concatenate(mid, axis=0) + bdot(jnp.concatenate([products, products], axis=1), w_prod_ref[...])
+        mid = jnp.concatenate(mid, axis=0) + bdot(jnp.concatenate([products, products], axis=1), w_prod[...])
         high, low = ksplit(channel_norm(mid))
         return mid, jnp.concatenate([high, low, high, low], axis=1)
 
     def transition(start, mid, normed):
-        hidden = ksplit(jnp.maximum(bdot(normed, w_up_ref[...]), 0.0))
-        down = bdot(jnp.concatenate(hidden, axis=1), w_down_ref[...])
+        hidden = ksplit(jnp.maximum(bdot(normed, w_ups[...]), 0.0))
+        down = bdot(jnp.concatenate(hidden, axis=1), w_downs[...])
         out = mid + (down[:, :lanes] + down[:, lanes:])
         out_ref[start : start + CHUNK_ROWS] = out.reshape((CHUNK_ROWS,) + out_ref.shape[1:])
 
@@ -267,23 +265,12 @@
         current = following
 
 
-def update_weights(w_outer, w_up, w_down):
-    p_high, p_low = split(w_outer[: w_outer.shape[0] // 2])
-    u_high, u_low = split(w_up)
-    down = jnp.concatenate(split(w_down), axis=1)
-    return (
-        jnp.concatenate([p_high, p_high, p_low, p_low], axis=0),
-        jnp.concatenate([u_high, u_high, u_low, u_low], axis=0),
-        jnp.concatenate([down, down], axis=0),
-    )
-
-
-def update_pair(place, pair, left, rights, w_diff, outer_bias, w_prod, w_up, w_down):
+def update_pair(place, pair, left, rights, w_outer, outer_bias, w_up, w_down):
     rows, cols, channels = pair.shape
     hidden = w_up.shape[1]
     whole = lambda x: pl.BlockSpec(x.shape, lambda s: (0,) * x.ndim)
     block = pl.BlockSpec((UPDATE_ROWS, cols, channels), lambda s: (s, 0, 0))
-    fixed = (left, *rights, w_diff, outer_bias[None, :], w_prod, w_up, w_down)
+    fixed = (left, *rights, w_outer, outer_bias[None, :], w_up, w_down)
     cells = rows * cols
     return pl.pallas_call(
         update_kernel,
@@ -295,6 +282,9 @@
             pltpu.VMEM((cols, channels), F32),
             pltpu.VMEM((cols, channels), F32),
             pltpu.VMEM((rows, channels), F32),
+            pltpu.VMEM((2 * w_outer.shape[0], channels), BF),
+            pltpu.VMEM((4 * channels, hidden), BF),
+            pltpu.VMEM((2 * hidden, 2 * channels), BF),
         ],
         compiler_params=pltpu.CompilerParams(vmem_limit_bytes=50 * MIB),
         cost_estimate=pl.CostEstimate(
@@ -319,6 +309,20 @@
     )(x, *others)
 
 
+def columns_first(n_row, n_col, other):
+    pairs = []
+    for k in range(n_col):
+        for half in range(2):
+            for core in range(2):
+                for plane in range(n_row // 4):
+                    x, y = HOPS[other][(plane - k) % (n_row // 4)]
+                    source = ((k // 2 + x) % (n_col // 2)) * 2 + ((k % 2) ^ y)
+                    pairs.append(
+                        (((k * 2 + (half ^ other)) * 2 + core) * n_col + source, ((plane * 2 + half) * 2 + core) * n_col + k)
+                    )
+    return sorted(pairs)
+
+
 def per_device(
     seq, query, key, value, pair, w_bias, w_out, w_left, w_right, w_outer, outer_bias, w_up, w_down
 ):
@@ -337,20 +341,18 @@
     queries = query[None]
     hop = 1
     while hop < n_col:
-        other = lax.ppermute(queries, "col", [(i, i ^ hop) for i in range(n_col)])
-        queries = jnp.concatenate([queries, other], axis=0)
+        if hop > 1:
+            queries = jnp.concatenate([queries, far_queries], axis=0)
+        far_queries = lax.ppermute(queries, "col", [(i, i ^ hop) for i in range(n_col)])
         hop *= 2
     pairs = [[z * 2 + k for z in range(n_row // 2)] for k in range(2)]
     own = lax.all_to_all(kv, "row", 0, 0, axis_index_groups=pairs)
-    bias = pair_bias(pair, w_bias)
-    weights = update_weights(w_outer, w_up, w_down)
-    w_out = jnp.concatenate(split(w_out), axis=1)
-    w_lr = jnp.concatenate([w_left, w_right], axis=1)
-    own = after(own, queries, bias, w_out, w_lr, *weights)
+    bias, bias_done = pair_bias(pair, w_bias)
+    own = after(own, far_queries[:1, :8], bias_done)
     across = [(i, i ^ 1) for i in range(n_row)]
     other = lax.ppermute(own, "row", across)
     place = jnp.stack([lax.axis_index("row") % 2, lax.axis_index("col")])
-    parts = attention(place, queries, own, other, bias)
+    parts = attention(place, queries, far_queries, own, other, bias)
     parts = lax.all_to_all(parts, "col", 0, 0)
 
     attn = pl.pallas_call(
@@ -368,20 +370,22 @@
         ),
         compiler_params=pltpu.CompilerParams(vmem_limit_bytes=8 * MIB),
         name="project",
-    )(attn, w_out, seq, w_lr)
+    )(attn, w_out, seq, w_left.T, w_right.T)
     shares = lax.all_to_all(shares, "col", 0, 0)
     left, right = pl.pallas_call(
         functools.partial(left_right_kernel, width),
         out_shape=(
             jax.ShapeDtypeStruct((rows, channels), F32),
-            jax.ShapeDtypeStruct((n_row // 2, rows // 2, channels), F32),
+            jax.ShapeDtypeStruct((rows // 2, channels), F32),
         ),
         compiler_params=pltpu.CompilerParams(vmem_limit_bytes=8 * MIB),
         name="left_right",
     )(shares)
-    right = lax.all_to_all(right, "row", 0, 0, axis_index_groups=pairs)
+    near, far = [lax.ppermute(right, ("row", "col"), columns_first(n_row, n_col, other)) for other in (0, 1)]
+    second = lax.axis_index("row") // 2 % 2 == 1
+    right = jnp.stack([jnp.where(second, far, near), jnp.where(second, near, far)])
     rights = (right, lax.ppermute(right, "row", across))
-    return seq_new, update_pair(place, pair, left, rights, w_outer[w_outer.shape[0] // 2 :], outer_bias, *weights)
+    return seq_new, update_pair(place, pair, left, rights, w_outer, outer_bias, w_up, w_down)
 
 
 def solution(mesh):

time: 117 us -> 105 us (0.90)
  blocking collectives: 44.4 us -> 26.8 us
  waiting for transfers between devices: 6.77 us -> 15.1 us
  other arithmetic: 5.56 us -> 1.57 us
  starting transfers between devices: 25.3 us -> 28.7 us
  local copies, waits for them, and re-layouts: 6.98 us -> 4.98 us
    all_to_all x1 -> x0, blocking collectives: 17.6 us -> none  [per_device(): right = lax.all_to_all(right, 'row', 0, 0, axis_index_groups=pairs)]
    ppermute x3 -> x5, waiting for transfers between devices: 2.52 us -> 8.57 us  [the longest x3 4.78 us: per_device(): lax.ppermute(queries, 'col', [(i, i ^ hop) for i in range(n_col)])]
    convert_element_type x4 -> x0, other arithmetic: 3.12 us -> none  [split(): return (high.astype(BF), (x - high).astype(BF))]
    all_to_all x1, waiting for transfers between devices: 1.22 us -> 3.83 us  [per_device(): own = lax.all_to_all(kv, 'row', 0, 0, axis_index_groups=pairs)]
    ppermute x3 -> x5, starting transfers between devices: 6.05 us -> 8.45 us  [the longest x3 4.44 us: per_device(): lax.ppermute(queries, 'col', [(i, i ^ hop) for i in range(n_col)])]
    unnamed x30 -> x20, local copies, waits for them, and re-layouts: 6.98 us -> 4.98 us
  transfers between devices with their start and end apart: 6 -> 8, of which waited for: 4 -> 7; matrix products, arithmetic and copies ran while one was open for 6% -> 1% of each run, Pallas kernels for 6% -> 4%
where the time goes in v3:
time: 105 us; the launch traced here: 104 us
  starting transfers between devices  28.7 us (27%)
  blocking collectives  26.8 us (26%)
  Pallas kernels  26.2 us (25%)
  waiting for transfers between devices  15.1 us (14%)
  local copies, waits for them, and re-layouts  4.98 us (5%)
  other arithmetic  1.57 us (1%)
    pallas_call x1, Pallas kernels, update_pair(): pl.pallas_call(update_kernel, grid=(rows // UPDATE_ROWS,), in_specs=[pl.B...  16.2 us
    all_to_all x1, starting transfers between devices, per_device(): own = lax.all_to_all(kv, 'row', 0, 0, axis_index_groups=pairs)  11.7 us
    all_to_all x1, blocking collectives, per_device(): parts = lax.all_to_all(parts, 'col', 0, 0)  9.87 us
    all_to_all x1, blocking collectives, per_device(): attn = lax.all_to_all(attn, 'col', 0, 0)  8.51 us
    all_to_all x1, blocking collectives, per_device(): shares = lax.all_to_all(shares, 'col', 0, 0)  8.45 us
    ppermute x1, starting transfers between devices, per_device(): rights = (right, lax.ppermute(right, 'row', across))  5.45 us
    unnamed x20, local copies, waits for them, and re-layouts  4.98 us
    ppermute x3, waiting for transfers between devices, per_device(): lax.ppermute(queries, 'col', [(i, i ^ hop) for i in range(n_col)])  4.78 us
  transfers between devices with their start and end apart: 8, of which 7 were waited for; matrix products, arithmetic and copies ran while one was open for 1% of the time, Pallas kernels for 4%

profile of v3, /device:TPU:1, one launch (start us, length us, event | category | flops | bytes accessed | tf_op | source)
XLA Modules:
  0.0 104.2 jit_solution(3388568515181666106)
XLA Ops:
  0.6 1.7 %pack.1 = f32[16,96,128]{2,1,0:T(8,128)} custom-call(f32[32,192]{1,0:T(8,128)} %bitcast.20, f32[32,192]{1,0:T(8,128)} %bitcast.21), custom_call_target="tpu_custom_call" | custom-call | tf_op jit(solution)/shard_map/pack/pallas_call | solution.py:336
  2.4 11.7 %all-to-all-start = ((f32[16,96,128]{2,1,0:T(8,128)}), f32[16,96,128]{2,1,0:T(8,128)S(1)}, u32[]{:S(2)}, u32[]{:S(2)}) async-start(f32[16,96,128]{2,1,0:T(8,128)} %pack.1), calls=%async_computation | async-start | bytes 1572864 | tf_op jit(solution)/shard_map/all_to_all | solution.py:349
  14.1 0.5 collective-permute-start
  14.6 2.8 %collective-permute-done = f32[1,48,128]{2,1,0:T(8,128)S(1)} collective-permute-done((f32[1,48,128]{2,1,0:T(8,128)}, f32[1,48,128]{2,1,0:T(8,128)S(1)}, u32[]{:S(2)}, u32[]{:S(2)}) %collective-permute-start) | collective-permute-done | bytes 24608 | tf_op jit(solution)/shard_map/ppermute | solution.py:346
  17.4 0.7 pad_maximum_fusion.1
  18.1 1.2 %collective-permute-start.1 = (f32[2,48,128]{2,1,0:T(8,128)S(1)}, f32[2,48,128]{2,1,0:T(8,128)S(1)}, u32[]{:S(2)}, u32[]{:S(2)}) collective-permute-start(f32[2,48,128]{2,1,0:T(8,128)S(1)} %pad_maximum_fusion.1), channel_id=1, source_target_pairs={{0,2},{1,3},{2,0},{3,1},{4,6},{5,7},{6,4},{7,5},{8,10},{9,11},{10,... | collective-permute-start | bytes 147464 | tf_op jit(solution)/shard_map/ppermute | solution.py:346
  19.3 2.0 %collective-permute-done.1 = f32[2,48,128]{2,1,0:T(8,128)S(1)} collective-permute-done((f32[2,48,128]{2,1,0:T(8,128)S(1)}, f32[2,48,128]{2,1,0:T(8,128)S(1)}, u32[]{:S(2)}, u32[]{:S(2)}) %collective-permute-start.1) | collective-permute-done | bytes 49184 | tf_op jit(solution)/shard_map/ppermute | solution.py:346
  21.3 0.7 pad_maximum_fusion.q_ref
  22.1 2.7 %collective-permute-start.2 = (f32[4,48,128]{2,1,0:T(8,128)S(1)}, f32[4,48,128]{2,1,0:T(8,128)S(1)}, u32[]{:S(2)}, u32[]{:S(2)}) collective-permute-start(f32[4,48,128]{2,1,0:T(8,128)S(1)} %pad_maximum_fusion.q_ref), channel_id=1, source_target_pairs={{0,4},{1,5},{2,6},{3,7},{4,0},{5,1},{6,2},{7,3},{8,12},{9,13},{10,... | collective-permute-start | bytes 294920 | tf_op jit(solution)/shard_map/ppermute | solution.py:346
  24.8 0.0 copy-start
  24.8 2.3 %copy-done = f32[48,192,128]{2,1,0:T(8,128)S(1)} copy-done((f32[48,192,128]{2,1,0:T(8,128)S(1)}, f32[48,192,128]{2,1,0:T(8,128)}, u32[]{:S(2)}) %copy-start) | copy-done | bytes 4718616
  27.2 0.0 copy-start.5
  27.2 0.7 copy-done.5
  27.9 0.0 copy-start.2
  27.9 0.0 copy-start.3
  27.9 0.0 copy-start.4
  27.9 4.7 %pair_bias.1 = (f32[32,48,192]{2,1,0:T(8,128)S(1)}, f32[8,128]{1,0:T(8,128)S(1)}) custom-call(f32[48,192,128]{2,1,0:T(8,128)S(1)} %copy-done, f32[32,128]{1,0:T(8,128)S(1)} %bitcast.15), custom_call_target="tpu_custom_call" | custom-call | flops 452984832 | bytes 5898240 | tf_op jit(solution)/shard_map/pair_bias/pallas_call | solution.py:125
  32.6 0.0 copy-start.8
  32.6 0.0 copy-start.9
  32.6 0.0 collective-permute-done.2.far_ref
  32.6 3.8 %all-to-all-done.refs_0_ = f32[16,96,128]{2,1,0:T(8,128)S(1)} async-done(((f32[16,96,128]{2,1,0:T(8,128)}), f32[16,96,128]{2,1,0:T(8,128)S(1)}, u32[]{:S(2)}, u32[]{:S(2)}) %all-to-all-start) | async-done | bytes 786464 | tf_op jit(solution)/shard_map/all_to_all | solution.py:349
  36.4 3.1 %collective-permute-start.3 = (f32[16,96,128]{2,1,0:T(8,128)S(1)}, f32[16,96,128]{2,1,0:T(8,128)S(1)}, u32[]{:S(2)}, u32[]{:S(2)}) collective-permute-start(f32[16,96,128]{2,1,0:T(8,128)S(1)} %after.1.own_ref), channel_id=1, source_target_pairs={{0,8},{8,0},{16,24},{24,16},{32,40},{40,32},{48,56},{56,48},{64,72... | collective-permute-start | bytes 2359304 | tf_op jit(solution)/shard_map/ppermute | solution.py:353
  39.5 0.0 copy-start.1
  39.5 0.1 pad_add_fusion.place_ref
  39.6 1.8 %collective-permute-done.3.other_ref = f32[16,96,128]{2,1,0:T(8,128)S(1)} collective-permute-done((f32[16,96,128]{2,1,0:T(8,128)S(1)}, f32[16,96,128]{2,1,0:T(8,128)S(1)}, u32[]{:S(2)}, u32[]{:S(2)}) %collective-permute-start.3) | collective-permute-done | bytes 786464 | tf_op jit(solution)/shard_map/ppermute | solution.py:353
  41.4 2.1 %attention.1 = f32[8,56,128]{2,1,0:T(8,128)S(1)} custom-call(s32[2]{0:T(128)S(1)} %pad_add_fusion.place_ref, f32[4,48,128]{2,1,0:T(8,128)S(1)} %pad_maximum_fusion.q_ref, f32[4,48,128]{2,1,0:T(8,128)S(1)} %collective-permute-done.2.far_ref, f32[16,96,128]{2,1,0:T(8,128)S(1)} %after.1.own_ref, f32[16,96,128]{2,1,0:T(8,128)S(1)} %collective-permute-done.3.other_ref, ...), custom_call_target="tpu_custom_call" | custom-call | tf_op jit(solution)/shard_map/attention/pallas_call | solution.py:200
  43.5 9.9 %all_to_all.20.parts_ref = f32[8,56,128]{2,1,0:T(8,128)S(1)} all-to-all(f32[8,56,128]{2,1,0:T(8,128)S(1)} %attention.1), channel_id=1, replica_groups=mesh['row'=32,'col'=8] {'col'}, dimensions={0} | all-to-all | bytes 458752 | tf_op jit(solution)/shard_map/all_to_all | solution.py:356
  53.4 0.5 merge.1
  53.8 8.5 %all_to_all.21.attn_ref = f32[8,48,128]{2,1,0:T(8,128)S(1)} all-to-all(f32[8,48,128]{2,1,0:T(8,128)S(1)} %merge.1), channel_id=1, replica_groups=mesh['row'=32,'col'=8] {'col'}, dimensions={0} | all-to-all | bytes 393216 | tf_op jit(solution)/shard_map/all_to_all | solution.py:364
  62.3 0.0 copy-done.2
  62.3 0.0 copy-done.3
  62.3 0.0 copy-done.4
  62.4 0.0 copy-done.1
  62.4 0.9 project.1
  63.2 8.5 %all_to_all.22.parts_ref = f32[8,56,128]{2,1,0:T(8,128)S(1)} all-to-all(f32[8,56,128]{2,1,0:T(8,128)S(1)} %get-tuple-element.11), channel_id=1, replica_groups=mesh['row'=32,'col'=8] {'col'}, dimensions={0} | all-to-all | bytes 458752 | tf_op jit(solution)/shard_map/all_to_all | solution.py:374
  71.7 0.3 left_right.1
  72.0 1.3 %collective-permute-start.5 = (f32[24,128]{1,0:T(8,128)S(1)}, f32[24,128]{1,0:T(8,128)S(1)}, u32[]{:S(2)}, u32[]{:S(2)}) collective-permute-start(f32[24,128]{1,0:T(8,128)S(1)} %get-tuple-element.13), channel_id=1, source_target_pairs={{0,128},{1,96},{2,160},{3,192},{4,224},{5,0},{6,64},{7,32},{8,136}... | collective-permute-start | bytes 36872 | tf_op jit(solution)/shard_map/ppermute | solution.py:384
  73.3 2.7 %collective-permute-start.4 = (f32[24,128]{1,0:T(8,128)S(1)}, f32[24,128]{1,0:T(8,128)S(1)}, u32[]{:S(2)}, u32[]{:S(2)}) collective-permute-start(f32[24,128]{1,0:T(8,128)S(1)} %get-tuple-element.13), channel_id=1, source_target_pairs={{0,112},{1,144},{2,48},{3,176},{4,16},{5,208},{6,240},{7,80},{8,12... | collective-permute-start | bytes 36872 | tf_op jit(solution)/shard_map/ppermute | solution.py:384
  76.0 1.0 collective-permute-done.5
  77.0 2.8 %collective-permute-done.4 = f32[24,128]{1,0:T(8,128)S(1)} collective-permute-done((f32[24,128]{1,0:T(8,128)S(1)}, f32[24,128]{1,0:T(8,128)S(1)}, u32[]{:S(2)}, u32[]{:S(2)}) %collective-permute-start.4) | collective-permute-done | bytes 12320 | tf_op jit(solution)/shard_map/ppermute | solution.py:384
  79.8 5.5 %collective-permute-start.6 = (f32[2,24,128]{2,1,0:T(8,128)S(1)}, f32[2,24,128]{2,1,0:T(8,128)S(1)}, u32[]{:S(2)}, u32[]{:S(2)}) collective-permute-start(f32[2,24,128]{2,1,0:T(8,128)S(1)} %pad_maximum_fusion.2.own_ref), channel_id=1, source_target_pairs={{0,8},{8,0},{16,24},{24,16},{32,40},{40,32},{48,56},{56,48},{64,72... | collective-permute-start | bytes 73736 | tf_op jit(solution)/shard_map/ppermute | solution.py:387
  85.2 0.8 collective-permute-done.6.other_ref
  86.1 0.0 copy-done.8
  86.1 0.0 copy-done.9
  86.1 0.0 copy-start.6
  86.1 0.9 copy-done.6
  87.0 0.9 copy-done.7
  88.0 16.2 %update_pair.1 = f32[48,192,128]{2,1,0:T(8,128)} custom-call(s32[2]{0:T(128)S(1)} %pad_add_fusion.place_ref, f32[48,192,128]{2,1,0:T(8,128)} %pair_ref.3, f32[48,128]{1,0:T(8,128)S(1)} %get-tuple-element.12.left_ref, f32[2,24,128]{2,1,0:T(8,128)S(1)} %pad_maximum_fusion.2.own_ref, f32[2,24,128]{2,1,0:T(8,128)S(1)} %collective-permute-done.6.other_ref, ...), custom_call_target="tpu_custom_call" | custom-call | flops 10267656192 | bytes 9437184 | tf_op jit(solution)/shard_map/update_pair/pallas_call | solution.py:275
  (5 shorter events, 0.0 us)
Async XLA Ops:
  2.4 34.1 %all-to-all-start = ((f32[16,96,128]{2,1,0:T(8,128)}), f32[16,96,128]{2,1,0:T(8,128)S(1)}, u32[]{:S(2)}, u32[]{:S(2)}) async-start(f32[16,96,128]{2,1,0:T(8,128)} %pack.1), calls=%async_computation | async-start | bytes 1572864 | tf_op jit(solution)/shard_map/all_to_all | solution.py:349
  14.1 3.2 %collective-permute-start = (f32[1,48,128]{2,1,0:T(8,128)}, f32[1,48,128]{2,1,0:T(8,128)S(1)}, u32[]{:S(2)}, u32[]{:S(2)}) collective-permute-start(f32[1,48,128]{2,1,0:T(8,128)} %bitcast.17), channel_id=1, source_target_pairs={{0,1},{1,0},{2,3},{3,2},{4,5},{5,4},{6,7},{7,6},{8,9},{9,8},{10,11... | collective-permute-start | bytes 73736 | tf_op jit(solution)/shard_map/ppermute | solution.py:346
  18.1 3.2 %collective-permute-start.1 = (f32[2,48,128]{2,1,0:T(8,128)S(1)}, f32[2,48,128]{2,1,0:T(8,128)S(1)}, u32[]{:S(2)}, u32[]{:S(2)}) collective-permute-start(f32[2,48,128]{2,1,0:T(8,128)S(1)} %pad_maximum_fusion.1), channel_id=1, source_target_pairs={{0,2},{1,3},{2,0},{3,1},{4,6},{5,7},{6,4},{7,5},{8,10},{9,11},{10,... | collective-permute-start | bytes 147464 | tf_op jit(solution)/shard_map/ppermute | solution.py:346
  22.1 10.5 %collective-permute-start.2 = (f32[4,48,128]{2,1,0:T(8,128)S(1)}, f32[4,48,128]{2,1,0:T(8,128)S(1)}, u32[]{:S(2)}, u32[]{:S(2)}) collective-permute-start(f32[4,48,128]{2,1,0:T(8,128)S(1)} %pad_maximum_fusion.q_ref), channel_id=1, source_target_pairs={{0,4},{1,5},{2,6},{3,7},{4,0},{5,1},{6,2},{7,3},{8,12},{9,13},{10,... | collective-permute-start | bytes 294920 | tf_op jit(solution)/shard_map/ppermute | solution.py:346
  24.8 2.3 %copy-start = (f32[48,192,128]{2,1,0:T(8,128)S(1)}, f32[48,192,128]{2,1,0:T(8,128)}, u32[]{:S(2)}) copy-start(f32[48,192,128]{2,1,0:T(8,128)} %pair_ref.3) | copy-start | bytes 14155780
  27.2 0.7 copy-start.5
  27.9 34.5 %copy-start.2 = (f32[128,64]{0,1:T(8,128)S(1)}, f32[128,64]{0,1:T(8,128)}, u32[]{:S(2)}) copy-start(f32[128,64]{0,1:T(8,128)} %param.20) | copy-start | bytes 98308
  27.9 34.5 %copy-start.3 = (f32[128,64]{0,1:T(8,128)S(1)}, f32[128,64]{0,1:T(8,128)}, u32[]{:S(2)}) copy-start(f32[128,64]{0,1:T(8,128)} %param.21) | copy-start | bytes 98308
  27.9 34.5 %copy-start.4 = (f32[48,128]{1,0:T(8,128)S(1)}, f32[48,128]{1,0:T(8,128)}, u32[]{:S(2)}) copy-start(f32[48,128]{1,0:T(8,128)} %seq_ref.1) | copy-start | bytes 73732
  32.6 53.5 %copy-start.8 = (f32[128,128]{1,0:T(8,128)S(1)}, f32[128,128]{1,0:T(8,128)}, u32[]{:S(2)}) copy-start(f32[128,128]{1,0:T(8,128)} %w_outer_ref.1) | copy-start | bytes 196612
  32.6 53.5 %copy-start.9 = (f32[128]{0:T(128)S(1)}, f32[128]{0:T(128)}, u32[]{:S(2)}) copy-start(f32[128]{0:T(128)} %param.23) | copy-start | bytes 1540
  36.4 5.0 %collective-permute-start.3 = (f32[16,96,128]{2,1,0:T(8,128)S(1)}, f32[16,96,128]{2,1,0:T(8,128)S(1)}, u32[]{:S(2)}, u32[]{:S(2)}) collective-permute-start(f32[16,96,128]{2,1,0:T(8,128)S(1)} %after.1.own_ref), channel_id=1, source_target_pairs={{0,8},{8,0},{16,24},{24,16},{32,40},{40,32},{48,56},{56,48},{64,72... | collective-permute-start | bytes 2359304 | tf_op jit(solution)/shard_map/ppermute | solution.py:353
  39.5 22.8 %copy-start.1 = (f32[1024,128]{1,0:T(8,128)S(1)}, f32[1024,128]{1,0:T(8,128)}, u32[]{:S(2)}) copy-start(f32[1024,128]{1,0:T(8,128)} %w_out_ref.1) | copy-start | bytes 1572868
  72.0 5.0 %collective-permute-start.5 = (f32[24,128]{1,0:T(8,128)S(1)}, f32[24,128]{1,0:T(8,128)S(1)}, u32[]{:S(2)}, u32[]{:S(2)}) collective-permute-start(f32[24,128]{1,0:T(8,128)S(1)} %get-tuple-element.13), channel_id=1, source_target_pairs={{0,128},{1,96},{2,160},{3,192},{4,224},{5,0},{6,64},{7,32},{8,136}... | collective-permute-start | bytes 36872 | tf_op jit(solution)/shard_map/ppermute | solution.py:384
  73.3 6.5 %collective-permute-start.4 = (f32[24,128]{1,0:T(8,128)S(1)}, f32[24,128]{1,0:T(8,128)S(1)}, u32[]{:S(2)}, u32[]{:S(2)}) collective-permute-start(f32[24,128]{1,0:T(8,128)S(1)} %get-tuple-element.13), channel_id=1, source_target_pairs={{0,112},{1,144},{2,48},{3,176},{4,16},{5,208},{6,240},{7,80},{8,12... | collective-permute-start | bytes 36872 | tf_op jit(solution)/shard_map/ppermute | solution.py:384
  79.8 6.3 %collective-permute-start.6 = (f32[2,24,128]{2,1,0:T(8,128)S(1)}, f32[2,24,128]{2,1,0:T(8,128)S(1)}, u32[]{:S(2)}, u32[]{:S(2)}) collective-permute-start(f32[2,24,128]{2,1,0:T(8,128)S(1)} %pad_maximum_fusion.2.own_ref), channel_id=1, source_target_pairs={{0,8},{8,0},{16,24},{24,16},{32,40},{40,32},{48,56},{56,48},{64,72... | collective-permute-start | bytes 73736 | tf_op jit(solution)/shard_map/ppermute | solution.py:387
  86.1 1.0 copy-start.6
  87.0 0.9 copy-start.7

commit v4 on v3

--- a/solution.py
+++ b/solution.py
@@ -286,7 +286,7 @@
             pltpu.VMEM((4 * channels, hidden), BF),
             pltpu.VMEM((2 * hidden, 2 * channels), BF),
         ],
-        compiler_params=pltpu.CompilerParams(vmem_limit_bytes=50 * MIB),
+        compiler_params=pltpu.CompilerParams(vmem_limit_bytes=57 * MIB),
         cost_estimate=pl.CostEstimate(
             flops=2 * cells * channels * (8 * hidden + 256),
             bytes_accessed=8 * cells * channels,

time: 105 us -> 104 us (level)
  transfers between devices with their start and end apart: 8 -> 8, of which waited for: 7 -> 7; matrix products, arithmetic and copies ran while one was open for 1% -> 2% of each run, Pallas kernels for 4% -> 4%
where the time goes in v4:
time: 104 us
  starting transfers between devices  28.6 us (28%)
  blocking collectives  26.8 us (26%)
  Pallas kernels  26.4 us (25%)
  waiting for transfers between devices  15.1 us (15%)
  local copies, waits for them, and re-layouts  4.29 us (4%)
  other arithmetic  1.57 us (2%)
    pallas_call x1, Pallas kernels, update_pair(): pl.pallas_call(update_kernel, grid=(rows // UPDATE_ROWS,), in_specs=[pl.B...  16.3 us
    all_to_all x1, starting transfers between devices, per_device(): own = lax.all_to_all(kv, 'row', 0, 0, axis_index_groups=pairs)  11.7 us
    all_to_all x1, blocking collectives, per_device(): parts = lax.all_to_all(parts, 'col', 0, 0)  9.87 us
    all_to_all x1, blocking collectives, per_device(): attn = lax.all_to_all(attn, 'col', 0, 0)  8.51 us
    all_to_all x1, blocking collectives, per_device(): shares = lax.all_to_all(shares, 'col', 0, 0)  8.45 us
    ppermute x1, starting transfers between devices, per_device(): rights = (right, lax.ppermute(right, 'row', across))  5.46 us
    ppermute x3, waiting for transfers between devices, per_device(): lax.ppermute(queries, 'col', [(i, i ^ hop) for i in range(n_col)])  4.78 us
    pallas_call x1, Pallas kernels, pair_bias(): pl.pallas_call(bias_kernel, grid=(rows // BIAS_ROWS,), in_specs=[block, p...  4.64 us
  transfers between devices with their start and end apart: 8, of which 7 were waited for; matrix products, arithmetic and copies ran while one was open for 2% of the time, Pallas kernels for 4%

profile of v4, /device:TPU:1, one launch (start us, length us, event | category | flops | bytes accessed | tf_op | source)
XLA Modules:
  0.0 103.6 jit_solution(11342317017385486459)
XLA Ops:
  0.6 1.7 %pack.1 = f32[16,96,128]{2,1,0:T(8,128)} custom-call(f32[32,192]{1,0:T(8,128)} %bitcast.19, f32[32,192]{1,0:T(8,128)} %bitcast.20), custom_call_target="tpu_custom_call" | custom-call | tf_op jit(solution)/shard_map/pack/pallas_call | solution.py:336
  2.4 11.7 %all-to-all-start = ((f32[16,96,128]{2,1,0:T(8,128)}), f32[16,96,128]{2,1,0:T(8,128)S(1)}, u32[]{:S(2)}, u32[]{:S(2)}) async-start(f32[16,96,128]{2,1,0:T(8,128)} %pack.1), calls=%async_computation | async-start | bytes 1572864 | tf_op jit(solution)/shard_map/all_to_all | solution.py:349
  14.1 0.5 collective-permute-start
  14.6 2.8 %collective-permute-done = f32[1,48,128]{2,1,0:T(8,128)S(1)} collective-permute-done((f32[1,48,128]{2,1,0:T(8,128)}, f32[1,48,128]{2,1,0:T(8,128)S(1)}, u32[]{:S(2)}, u32[]{:S(2)}) %collective-permute-start) | collective-permute-done | bytes 24608 | tf_op jit(solution)/shard_map/ppermute | solution.py:346
  17.4 0.7 pad_maximum_fusion.1
  18.1 1.2 %collective-permute-start.1 = (f32[2,48,128]{2,1,0:T(8,128)S(1)}, f32[2,48,128]{2,1,0:T(8,128)S(1)}, u32[]{:S(2)}, u32[]{:S(2)}) collective-permute-start(f32[2,48,128]{2,1,0:T(8,128)S(1)} %pad_maximum_fusion.1), channel_id=1, source_target_pairs={{0,2},{1,3},{2,0},{3,1},{4,6},{5,7},{6,4},{7,5},{8,10},{9,11},{10,... | collective-permute-start | bytes 147464 | tf_op jit(solution)/shard_map/ppermute | solution.py:346
  19.3 2.0 %collective-permute-done.1 = f32[2,48,128]{2,1,0:T(8,128)S(1)} collective-permute-done((f32[2,48,128]{2,1,0:T(8,128)S(1)}, f32[2,48,128]{2,1,0:T(8,128)S(1)}, u32[]{:S(2)}, u32[]{:S(2)}) %collective-permute-start.1) | collective-permute-done | bytes 49184 | tf_op jit(solution)/shard_map/ppermute | solution.py:346
  21.3 0.7 pad_maximum_fusion.q_ref
  22.1 2.7 %collective-permute-start.2 = (f32[4,48,128]{2,1,0:T(8,128)S(1)}, f32[4,48,128]{2,1,0:T(8,128)S(1)}, u32[]{:S(2)}, u32[]{:S(2)}) collective-permute-start(f32[4,48,128]{2,1,0:T(8,128)S(1)} %pad_maximum_fusion.q_ref), channel_id=1, source_target_pairs={{0,4},{1,5},{2,6},{3,7},{4,0},{5,1},{6,2},{7,3},{8,12},{9,13},{10,... | collective-permute-start | bytes 294920 | tf_op jit(solution)/shard_map/ppermute | solution.py:346
  24.8 0.0 copy-start
  24.8 2.3 %copy-done = f32[48,192,128]{2,1,0:T(8,128)S(1)} copy-done((f32[48,192,128]{2,1,0:T(8,128)S(1)}, f32[48,192,128]{2,1,0:T(8,128)}, u32[]{:S(2)}) %copy-start) | copy-done | bytes 4718616
  27.2 0.0 copy-start.5
  27.2 0.7 copy-done.5
  27.9 0.0 copy-start.2
  27.9 0.0 copy-start.3
  27.9 0.0 copy-start.4
  27.9 4.6 %pair_bias.1 = (f32[32,48,192]{2,1,0:T(8,128)S(1)}, f32[8,128]{1,0:T(8,128)S(1)}) custom-call(f32[48,192,128]{2,1,0:T(8,128)S(1)} %copy-done, f32[32,128]{1,0:T(8,128)S(1)} %bitcast.15), custom_call_target="tpu_custom_call" | custom-call | flops 452984832 | bytes 5898240 | tf_op jit(solution)/shard_map/pair_bias/pallas_call | solution.py:125
  32.6 0.0 collective-permute-done.2.far_ref
  32.6 3.9 %all-to-all-done.refs_0_ = f32[16,96,128]{2,1,0:T(8,128)S(1)} async-done(((f32[16,96,128]{2,1,0:T(8,128)}), f32[16,96,128]{2,1,0:T(8,128)S(1)}, u32[]{:S(2)}, u32[]{:S(2)}) %all-to-all-start) | async-done | bytes 786464 | tf_op jit(solution)/shard_map/all_to_all | solution.py:349
  36.4 3.1 %collective-permute-start.3 = (f32[16,96,128]{2,1,0:T(8,128)S(1)}, f32[16,96,128]{2,1,0:T(8,128)S(1)}, u32[]{:S(2)}, u32[]{:S(2)}) collective-permute-start(f32[16,96,128]{2,1,0:T(8,128)S(1)} %after.1.own_ref), channel_id=1, source_target_pairs={{0,8},{8,0},{16,24},{24,16},{32,40},{40,32},{48,56},{56,48},{64,72... | collective-permute-start | bytes 2359304 | tf_op jit(solution)/shard_map/ppermute | solution.py:353
  39.5 0.0 copy-start.1
  39.5 0.1 pad_add_fusion.place_ref
  39.6 0.0 copy-start.6
  39.6 1.8 %collective-permute-done.3.other_ref = f32[16,96,128]{2,1,0:T(8,128)S(1)} collective-permute-done((f32[16,96,128]{2,1,0:T(8,128)S(1)}, f32[16,96,128]{2,1,0:T(8,128)S(1)}, u32[]{:S(2)}, u32[]{:S(2)}) %collective-permute-start.3) | collective-permute-done | bytes 786464 | tf_op jit(solution)/shard_map/ppermute | solution.py:353
  41.4 2.1 %attention.1 = f32[8,56,128]{2,1,0:T(8,128)S(1)} custom-call(s32[2]{0:T(128)S(1)} %pad_add_fusion.place_ref, f32[4,48,128]{2,1,0:T(8,128)S(1)} %pad_maximum_fusion.q_ref, f32[4,48,128]{2,1,0:T(8,128)S(1)} %collective-permute-done.2.far_ref, f32[16,96,128]{2,1,0:T(8,128)S(1)} %after.1.own_ref, f32[16,96,128]{2,1,0:T(8,128)S(1)} %collective-permute-done.3.other_ref, ...), custom_call_target="tpu_custom_call" | custom-call | tf_op jit(solution)/shard_map/attention/pallas_call | solution.py:200
  43.6 9.9 %all_to_all.20.parts_ref = f32[8,56,128]{2,1,0:T(8,128)S(1)} all-to-all(f32[8,56,128]{2,1,0:T(8,128)S(1)} %attention.1), channel_id=1, replica_groups=mesh['row'=32,'col'=8] {'col'}, dimensions={0} | all-to-all | bytes 458752 | tf_op jit(solution)/shard_map/all_to_all | solution.py:356
  53.4 0.5 merge.1
  53.9 8.5 %all_to_all.21.attn_ref = f32[8,48,128]{2,1,0:T(8,128)S(1)} all-to-all(f32[8,48,128]{2,1,0:T(8,128)S(1)} %merge.1), channel_id=1, replica_groups=mesh['row'=32,'col'=8] {'col'}, dimensions={0} | all-to-all | bytes 393216 | tf_op jit(solution)/shard_map/all_to_all | solution.py:364
  62.4 0.0 copy-done.2
  62.4 0.0 copy-done.3
  62.4 0.0 copy-done.4
  62.4 0.0 copy-done.1
  62.4 0.9 project.1
  63.3 8.4 %all_to_all.22.parts_ref = f32[8,56,128]{2,1,0:T(8,128)S(1)} all-to-all(f32[8,56,128]{2,1,0:T(8,128)S(1)} %get-tuple-element.11), channel_id=1, replica_groups=mesh['row'=32,'col'=8] {'col'}, dimensions={0} | all-to-all | bytes 458752 | tf_op jit(solution)/shard_map/all_to_all | solution.py:374
  71.7 0.3 left_right.1
  72.0 0.0 copy-start.7
  72.0 0.6 copy-done.7
  72.6 1.3 %collective-permute-start.5 = (f32[24,128]{1,0:T(8,128)S(1)}, f32[24,128]{1,0:T(8,128)S(1)}, u32[]{:S(2)}, u32[]{:S(2)}) collective-permute-start(f32[24,128]{1,0:T(8,128)S(1)} %get-tuple-element.13), channel_id=1, source_target_pairs={{0,128},{1,96},{2,160},{3,192},{4,224},{5,0},{6,64},{7,32},{8,136}... | collective-permute-start | bytes 36872 | tf_op jit(solution)/shard_map/ppermute | solution.py:384
  73.9 2.6 %collective-permute-start.4 = (f32[24,128]{1,0:T(8,128)S(1)}, f32[24,128]{1,0:T(8,128)S(1)}, u32[]{:S(2)}, u32[]{:S(2)}) collective-permute-start(f32[24,128]{1,0:T(8,128)S(1)} %get-tuple-element.13), channel_id=1, source_target_pairs={{0,112},{1,144},{2,48},{3,176},{4,16},{5,208},{6,240},{7,80},{8,12... | collective-permute-start | bytes 36872 | tf_op jit(solution)/shard_map/ppermute | solution.py:384
  76.5 1.0 %collective-permute-done.5 = f32[24,128]{1,0:T(8,128)S(1)} collective-permute-done((f32[24,128]{1,0:T(8,128)S(1)}, f32[24,128]{1,0:T(8,128)S(1)}, u32[]{:S(2)}, u32[]{:S(2)}) %collective-permute-start.5) | collective-permute-done | bytes 12320 | tf_op jit(solution)/shard_map/ppermute | solution.py:384
  77.6 2.8 %collective-permute-done.4 = f32[24,128]{1,0:T(8,128)S(1)} collective-permute-done((f32[24,128]{1,0:T(8,128)S(1)}, f32[24,128]{1,0:T(8,128)S(1)}, u32[]{:S(2)}, u32[]{:S(2)}) %collective-permute-start.4) | collective-permute-done | bytes 12320 | tf_op jit(solution)/shard_map/ppermute | solution.py:384
  80.4 0.0 copy-start.8
  80.4 5.5 %collective-permute-start.6 = (f32[2,24,128]{2,1,0:T(8,128)S(1)}, f32[2,24,128]{2,1,0:T(8,128)S(1)}, u32[]{:S(2)}, u32[]{:S(2)}) collective-permute-start(f32[2,24,128]{2,1,0:T(8,128)S(1)} %pad_maximum_fusion.2.own_ref), channel_id=1, source_target_pairs={{0,8},{8,0},{16,24},{24,16},{32,40},{40,32},{48,56},{56,48},{64,72... | collective-permute-start | bytes 73736 | tf_op jit(solution)/shard_map/ppermute | solution.py:387
  85.8 0.8 collective-permute-done.6.other_ref
  86.7 0.0 copy-done.6
  86.7 0.0 copy-done.8
  86.7 0.6 copy-done.9
  87.3 16.3 %update_pair.1 = f32[48,192,128]{2,1,0:T(8,128)} custom-call(s32[2]{0:T(128)} %copy-done.6, f32[48,192,128]{2,1,0:T(8,128)} %pair_ref.3, f32[48,128]{1,0:T(8,128)} %copy-done.7, f32[2,24,128]{2,1,0:T(8,128)} %copy-done.8, f32[2,24,128]{2,1,0:T(8,128)} %copy-done.9, f32[128,128]{1,0:T(8,128)} %w_outer_ref.1, f32[1,128]{1,0:T(1,128)} %bitcast.21, ...), custom_call_target="tpu_custom_call" | custom-call | flops 10267656192 | bytes 9437184 | tf_op jit(solution)/shard_map/update_pair/pallas_call | solution.py:275
  (5 shorter events, 0.0 us)
Async XLA Ops:
  2.4 34.1 %all-to-all-start = ((f32[16,96,128]{2,1,0:T(8,128)}), f32[16,96,128]{2,1,0:T(8,128)S(1)}, u32[]{:S(2)}, u32[]{:S(2)}) async-start(f32[16,96,128]{2,1,0:T(8,128)} %pack.1), calls=%async_computation | async-start | bytes 1572864 | tf_op jit(solution)/shard_map/all_to_all | solution.py:349
  14.1 3.2 %collective-permute-start = (f32[1,48,128]{2,1,0:T(8,128)}, f32[1,48,128]{2,1,0:T(8,128)S(1)}, u32[]{:S(2)}, u32[]{:S(2)}) collective-permute-start(f32[1,48,128]{2,1,0:T(8,128)} %bitcast.16), channel_id=1, source_target_pairs={{0,1},{1,0},{2,3},{3,2},{4,5},{5,4},{6,7},{7,6},{8,9},{9,8},{10,11... | collective-permute-start | bytes 73736 | tf_op jit(solution)/shard_map/ppermute | solution.py:346
  18.1 3.2 %collective-permute-start.1 = (f32[2,48,128]{2,1,0:T(8,128)S(1)}, f32[2,48,128]{2,1,0:T(8,128)S(1)}, u32[]{:S(2)}, u32[]{:S(2)}) collective-permute-start(f32[2,48,128]{2,1,0:T(8,128)S(1)} %pad_maximum_fusion.1), channel_id=1, source_target_pairs={{0,2},{1,3},{2,0},{3,1},{4,6},{5,7},{6,4},{7,5},{8,10},{9,11},{10,... | collective-permute-start | bytes 147464 | tf_op jit(solution)/shard_map/ppermute | solution.py:346
  22.1 10.5 %collective-permute-start.2 = (f32[4,48,128]{2,1,0:T(8,128)S(1)}, f32[4,48,128]{2,1,0:T(8,128)S(1)}, u32[]{:S(2)}, u32[]{:S(2)}) collective-permute-start(f32[4,48,128]{2,1,0:T(8,128)S(1)} %pad_maximum_fusion.q_ref), channel_id=1, source_target_pairs={{0,4},{1,5},{2,6},{3,7},{4,0},{5,1},{6,2},{7,3},{8,12},{9,13},{10,... | collective-permute-start | bytes 294920 | tf_op jit(solution)/shard_map/ppermute | solution.py:346
  24.8 2.3 %copy-start = (f32[48,192,128]{2,1,0:T(8,128)S(1)}, f32[48,192,128]{2,1,0:T(8,128)}, u32[]{:S(2)}) copy-start(f32[48,192,128]{2,1,0:T(8,128)} %pair_ref.3) | copy-start | bytes 14155780
  27.2 0.7 copy-start.5
  27.9 34.5 %copy-start.2 = (f32[128,64]{0,1:T(8,128)S(1)}, f32[128,64]{0,1:T(8,128)}, u32[]{:S(2)}) copy-start(f32[128,64]{0,1:T(8,128)} %param.20) | copy-start | bytes 98308
  27.9 34.5 %copy-start.3 = (f32[128,64]{0,1:T(8,128)S(1)}, f32[128,64]{0,1:T(8,128)}, u32[]{:S(2)}) copy-start(f32[128,64]{0,1:T(8,128)} %param.21) | copy-start | bytes 98308
  27.9 34.5 %copy-start.4 = (f32[48,128]{1,0:T(8,128)S(1)}, f32[48,128]{1,0:T(8,128)}, u32[]{:S(2)}) copy-start(f32[48,128]{1,0:T(8,128)} %seq_ref.1) | copy-start | bytes 73732
  36.4 5.0 %collective-permute-start.3 = (f32[16,96,128]{2,1,0:T(8,128)S(1)}, f32[16,96,128]{2,1,0:T(8,128)S(1)}, u32[]{:S(2)}, u32[]{:S(2)}) collective-permute-start(f32[16,96,128]{2,1,0:T(8,128)S(1)} %after.1.own_ref), channel_id=1, source_target_pairs={{0,8},{8,0},{16,24},{24,16},{32,40},{40,32},{48,56},{56,48},{64,72... | collective-permute-start | bytes 2359304 | tf_op jit(solution)/shard_map/ppermute | solution.py:353
  39.5 22.9 %copy-start.1 = (f32[1024,128]{1,0:T(8,128)S(1)}, f32[1024,128]{1,0:T(8,128)}, u32[]{:S(2)}) copy-start(f32[1024,128]{1,0:T(8,128)} %w_out_ref.1) | copy-start | bytes 1572868
  39.6 47.1 %copy-start.6 = (s32[2]{0:T(128)}, s32[2]{0:T(128)S(1)}, u32[]{:S(2)}) copy-start(s32[2]{0:T(128)S(1)} %pad_add_fusion.place_ref) | copy-start | bytes 28
  72.0 0.6 copy-start.7
  72.6 4.9 %collective-permute-start.5 = (f32[24,128]{1,0:T(8,128)S(1)}, f32[24,128]{1,0:T(8,128)S(1)}, u32[]{:S(2)}, u32[]{:S(2)}) collective-permute-start(f32[24,128]{1,0:T(8,128)S(1)} %get-tuple-element.13), channel_id=1, source_target_pairs={{0,128},{1,96},{2,160},{3,192},{4,224},{5,0},{6,64},{7,32},{8,136}... | collective-permute-start | bytes 36872 | tf_op jit(solution)/shard_map/ppermute | solution.py:384
  73.9 6.5 %collective-permute-start.4 = (f32[24,128]{1,0:T(8,128)S(1)}, f32[24,128]{1,0:T(8,128)S(1)}, u32[]{:S(2)}, u32[]{:S(2)}) collective-permute-start(f32[24,128]{1,0:T(8,128)S(1)} %get-tuple-element.13), channel_id=1, source_target_pairs={{0,112},{1,144},{2,48},{3,176},{4,16},{5,208},{6,240},{7,80},{8,12... | collective-permute-start | bytes 36872 | tf_op jit(solution)/shard_map/ppermute | solution.py:384
  80.4 6.3 %copy-start.8 = (f32[2,24,128]{2,1,0:T(8,128)}, f32[2,24,128]{2,1,0:T(8,128)S(1)}, u32[]{:S(2)}) copy-start(f32[2,24,128]{2,1,0:T(8,128)S(1)} %pad_maximum_fusion.2.own_ref) | copy-start | bytes 73732
  80.4 6.3 %collective-permute-start.6 = (f32[2,24,128]{2,1,0:T(8,128)S(1)}, f32[2,24,128]{2,1,0:T(8,128)S(1)}, u32[]{:S(2)}, u32[]{:S(2)}) collective-permute-start(f32[2,24,128]{2,1,0:T(8,128)S(1)} %pad_maximum_fusion.2.own_ref), channel_id=1, source_target_pairs={{0,8},{8,0},{16,24},{24,16},{32,40},{40,32},{48,56},{56,48},{64,72... | collective-permute-start | bytes 73736 | tf_op jit(solution)/shard_map/ppermute | solution.py:387
  86.7 0.6 copy-start.9

commit v5 on v4

--- a/solution.py
+++ b/solution.py
@@ -12,7 +12,6 @@
 BF = jnp.bfloat16
 F32 = jnp.float32
 BIAS_ROWS = 16
-UPDATE_ROWS = 24
 CHUNK_ROWS = 4
 MIB = 2**20
 HOPS = (
@@ -208,45 +207,55 @@
 
 def update_kernel(
     place_ref, pair_ref, left_ref, own_ref, other_ref, w_outer_ref, bias_ref, w_up_ref, w_down_ref, out_ref,
-    rights, base, diffs, w_prod, w_ups, w_downs,
+    rights, base, diffs, w_prod, w_ups, w_downs, pairs, news, loaded, stored,
 ):
-    step = pl.program_id(0)
-    steps, _, lanes = pair_ref.shape
-
-    @pl.when(step == 0)
-    def _():
-        w_diff = w_outer_ref[lanes // 2 :, :]
-        half = own_ref.shape[1]
-        first = lax.broadcasted_iota(jnp.int32, (half, lanes), 1) < lanes // 2
-        even = place_ref[0] == 0
-        blocks = []
-        for p in range(rights.shape[0] // (4 * half)):
-            own, other = own_ref[p], other_ref[p]
-            blocks += [jnp.where(even, own, other), jnp.where(even, other, own)]
-        for block, packed in enumerate(blocks):
-            swapped = pltpu.roll(packed, lanes // 2, 1)
-            start = 2 * half * block
-            rights[start : start + half, :] = jnp.where(first, packed, swapped)
-            rights[start + half : start + 2 * half, :] = jnp.where(first, swapped, packed)
-        base[...] = bias_ref[...] - dot(rights[:, : lanes // 2], w_diff)
-        diffs[...] = dot(left_ref[:, : lanes // 2], w_diff)
-        high, low = ksplit(w_outer_ref[: lanes // 2, :])
-        w_prod[...] = jnp.concatenate([high, high, low, low], axis=0)
-        high, low = ksplit(w_up_ref[...])
-        w_ups[...] = jnp.concatenate([high, high, low, low], axis=0)
-        both = jnp.concatenate(ksplit(w_down_ref[...]), axis=1)
-        w_downs[...] = jnp.concatenate([both, both], axis=0)
+    rows, _, lanes = pair_ref.shape
+    starts = range(0, rows, CHUNK_ROWS)
+
+    def chunk(start):
+        return pl.ds(start, CHUNK_ROWS)
+
+    loads = [
+        pltpu.make_async_copy(pair_ref.at[chunk(s)], pairs.at[chunk(s)], loaded.at[k]) for k, s in enumerate(starts)
+    ]
+    stores = [
+        pltpu.make_async_copy(news.at[chunk(s)], out_ref.at[chunk(s)], stored.at[k]) for k, s in enumerate(starts)
+    ]
+    for load in loads:
+        load.start()
+
+    w_diff = w_outer_ref[lanes // 2 :, :]
+    half = own_ref.shape[1]
+    first = lax.broadcasted_iota(jnp.int32, (half, lanes), 1) < lanes // 2
+    even = place_ref[0] == 0
+    blocks = []
+    for p in range(rights.shape[0] // (4 * half)):
+        own, other = own_ref[p], other_ref[p]
+        blocks += [jnp.where(even, own, other), jnp.where(even, other, own)]
+    for block, packed in enumerate(blocks):
+        swapped = pltpu.roll(packed, lanes // 2, 1)
+        start = 2 * half * block
+        rights[start : start + half, :] = jnp.where(first, packed, swapped)
+        rights[start + half : start + 2 * half, :] = jnp.where(first, swapped, packed)
+    base[...] = bias_ref[...] - dot(rights[:, : lanes // 2], w_diff)
+    diffs[...] = dot(left_ref[:, : lanes // 2], w_diff)
+    high, low = ksplit(w_outer_ref[: lanes // 2, :])
+    w_prod[...] = jnp.concatenate([high, high, low, low], axis=0)
+    high, low = ksplit(w_up_ref[...])
+    w_ups[...] = jnp.concatenate([high, high, low, low], axis=0)
+    both = jnp.concatenate(ksplit(w_down_ref[...]), axis=1)
+    w_downs[...] = jnp.concatenate([both, both], axis=0)
 
     first = lax.broadcasted_iota(jnp.int32, base.shape, 1) < lanes // 2
 
     def normalize(start):
         products, mid = [], []
-        for r in range(start, start + CHUNK_ROWS):
-            i = step * steps + r
-            product = rights[...] * left_ref[pl.ds(i, 1), :]
+        loads[start // CHUNK_ROWS].wait()
+        for i in range(start, start + CHUNK_ROWS):
+            product = rights[...] * left_ref[i : i + 1, :]
             high = product.astype(BF).astype(F32)
             products.append(jnp.where(first, high, product - high).astype(BF))
-            mid.append(pair_ref[r] + (base[...] + diffs[pl.ds(i, 1), :]))
+            mid.append(pairs[i] + (base[...] + diffs[i : i + 1, :]))
         products = jnp.concatenate(products, axis=0)
         mid = jnp.concatenate(mid, axis=0) + bdot(jnp.concatenate([products, products], axis=1), w_prod[...])
         high, low = ksplit(channel_norm(mid))
@@ -256,25 +265,28 @@
         hidden = ksplit(jnp.maximum(bdot(normed, w_ups[...]), 0.0))
         down = bdot(jnp.concatenate(hidden, axis=1), w_downs[...])
         out = mid + (down[:, :lanes] + down[:, lanes:])
-        out_ref[start : start + CHUNK_ROWS] = out.reshape((CHUNK_ROWS,) + out_ref.shape[1:])
+        news[start : start + CHUNK_ROWS] = out.reshape((CHUNK_ROWS,) + out_ref.shape[1:])
+        stores[start // CHUNK_ROWS].start()
 
     current = normalize(0)
-    for start in range(0, steps, CHUNK_ROWS):
-        following = normalize(start + CHUNK_ROWS) if start + CHUNK_ROWS < steps else None
+    for start in starts:
+        following = normalize(start + CHUNK_ROWS) if start + CHUNK_ROWS < rows else None
         transition(start, *current)
         current = following
+    for store in stores:
+        store.wait()
 
 
 def update_pair(place, pair, left, rights, w_outer, outer_bias, w_up, w_down):
     rows, cols, channels = pair.shape
     hidden = w_up.shape[1]
     whole = lambda x: pl.BlockSpec(x.shape, lambda s: (0,) * x.ndim)
-    block = pl.BlockSpec((UPDATE_ROWS, cols, channels), lambda s: (s, 0, 0))
+    block = pl.BlockSpec(memory_space=pl.ANY)
     fixed = (left, *rights, w_outer, outer_bias[None, :], w_up, w_down)
     cells = rows * cols
     return pl.pallas_call(
         update_kernel,
-        grid=(rows // UPDATE_ROWS,),
+        grid=(1,),
         in_specs=[pl.BlockSpec(memory_space=pltpu.SMEM), block] + [whole(x) for x in fixed],
         out_specs=block,
         out_shape=jax.ShapeDtypeStruct(pair.shape, F32),
@@ -285,6 +297,10 @@
             pltpu.VMEM((2 * w_outer.shape[0], channels), BF),
             pltpu.VMEM((4 * channels, hidden), BF),
             pltpu.VMEM((2 * hidden, 2 * channels), BF),
+            pltpu.VMEM(pair.shape, F32),
+            pltpu.VMEM(pair.shape, F32),
+            pltpu.SemaphoreType.DMA((rows // CHUNK_ROWS,)),
+            pltpu.SemaphoreType.DMA((rows // CHUNK_ROWS,)),
         ],
         compiler_params=pltpu.CompilerParams(vmem_limit_bytes=57 * MIB),
         cost_estimate=pl.CostEstimate(

time: 104 us -> 110 us (1.058)
  Pallas kernels: 26.4 us -> 32.5 us
    pallas_call x1, Pallas kernels: 16.3 us -> 22.4 us  [update_pair(): pl.pallas_call(update_kernel, grid=(1,), in_specs=[pl.BlockSpec(memory_sp...]
  transfers between devices with their start and end apart: 8 -> 8, of which waited for: 7 -> 7; matrix products, arithmetic and copies ran while one was open for 2% -> 1% of each run, Pallas kernels for 4% -> 4%
where the time goes in v5:
time: 110 us
  Pallas kernels  32.5 us (30%)
  starting transfers between devices  28.6 us (26%)
  blocking collectives  26.8 us (24%)
  waiting for transfers between devices  15.1 us (14%)
  local copies, waits for them, and re-layouts  4.29 us (4%)
  other arithmetic  1.57 us (1%)
    pallas_call x1, Pallas kernels, update_pair(): pl.pallas_call(update_kernel, grid=(1,), in_specs=[pl.BlockSpec(memory_sp...  22.4 us
    all_to_all x1, starting transfers between devices, per_device(): own = lax.all_to_all(kv, 'row', 0, 0, axis_index_groups=pairs)  11.7 us
    all_to_all x1, blocking collectives, per_device(): parts = lax.all_to_all(parts, 'col', 0, 0)  9.87 us
    all_to_all x1, blocking collectives, per_device(): attn = lax.all_to_all(attn, 'col', 0, 0)  8.51 us
    all_to_all x1, blocking collectives, per_device(): shares = lax.all_to_all(shares, 'col', 0, 0)  8.45 us
    ppermute x1, starting transfers between devices, per_device(): rights = (right, lax.ppermute(right, 'row', across))  5.46 us
    ppermute x3, waiting for transfers between devices, per_device(): lax.ppermute(queries, 'col', [(i, i ^ hop) for i in range(n_col)])  4.78 us
    pallas_call x1, Pallas kernels, pair_bias(): pl.pallas_call(bias_kernel, grid=(rows // BIAS_ROWS,), in_specs=[block, p...  4.64 us
  transfers between devices with their start and end apart: 8, of which 7 were waited for; matrix products, arithmetic and copies ran while one was open for 1% of the time, Pallas kernels for 4%

profile of v5, /device:TPU:1, one launch (start us, length us, event | category | flops | bytes accessed | tf_op | source)
XLA Modules:
  0.0 109.9 jit_solution(6550611442181692593)
XLA Ops:
  0.6 1.7 %pack.1 = f32[16,96,128]{2,1,0:T(8,128)} custom-call(f32[32,192]{1,0:T(8,128)} %bitcast.19, f32[32,192]{1,0:T(8,128)} %bitcast.20), custom_call_target="tpu_custom_call" | custom-call | tf_op jit(solution)/shard_map/pack/pallas_call | solution.py:352
  2.4 11.7 %all-to-all-start = ((f32[16,96,128]{2,1,0:T(8,128)}), f32[16,96,128]{2,1,0:T(8,128)S(1)}, u32[]{:S(2)}, u32[]{:S(2)}) async-start(f32[16,96,128]{2,1,0:T(8,128)} %pack.1), calls=%async_computation | async-start | bytes 1572864 | tf_op jit(solution)/shard_map/all_to_all | solution.py:365
  14.1 0.5 collective-permute-start
  14.6 2.8 %collective-permute-done = f32[1,48,128]{2,1,0:T(8,128)S(1)} collective-permute-done((f32[1,48,128]{2,1,0:T(8,128)}, f32[1,48,128]{2,1,0:T(8,128)S(1)}, u32[]{:S(2)}, u32[]{:S(2)}) %collective-permute-start) | collective-permute-done | bytes 24608 | tf_op jit(solution)/shard_map/ppermute | solution.py:362
  17.4 0.7 pad_maximum_fusion.1
  18.1 1.2 %collective-permute-start.1 = (f32[2,48,128]{2,1,0:T(8,128)S(1)}, f32[2,48,128]{2,1,0:T(8,128)S(1)}, u32[]{:S(2)}, u32[]{:S(2)}) collective-permute-start(f32[2,48,128]{2,1,0:T(8,128)S(1)} %pad_maximum_fusion.1), channel_id=1, source_target_pairs={{0,2},{1,3},{2,0},{3,1},{4,6},{5,7},{6,4},{7,5},{8,10},{9,11},{10,... | collective-permute-start | bytes 147464 | tf_op jit(solution)/shard_map/ppermute | solution.py:362
  19.3 2.0 %collective-permute-done.1 = f32[2,48,128]{2,1,0:T(8,128)S(1)} collective-permute-done((f32[2,48,128]{2,1,0:T(8,128)S(1)}, f32[2,48,128]{2,1,0:T(8,128)S(1)}, u32[]{:S(2)}, u32[]{:S(2)}) %collective-permute-start.1) | collective-permute-done | bytes 49184 | tf_op jit(solution)/shard_map/ppermute | solution.py:362
  21.3 0.7 pad_maximum_fusion.q_ref
  22.1 2.7 %collective-permute-start.2 = (f32[4,48,128]{2,1,0:T(8,128)S(1)}, f32[4,48,128]{2,1,0:T(8,128)S(1)}, u32[]{:S(2)}, u32[]{:S(2)}) collective-permute-start(f32[4,48,128]{2,1,0:T(8,128)S(1)} %pad_maximum_fusion.q_ref), channel_id=1, source_target_pairs={{0,4},{1,5},{2,6},{3,7},{4,0},{5,1},{6,2},{7,3},{8,12},{9,13},{10,... | collective-permute-start | bytes 294920 | tf_op jit(solution)/shard_map/ppermute | solution.py:362
  24.8 0.0 copy-start
  24.8 2.3 %copy-done = f32[48,192,128]{2,1,0:T(8,128)S(1)} copy-done((f32[48,192,128]{2,1,0:T(8,128)S(1)}, f32[48,192,128]{2,1,0:T(8,128)}, u32[]{:S(2)}) %copy-start) | copy-done | bytes 4718616
  27.2 0.0 copy-start.5
  27.2 0.7 copy-done.5
  27.9 0.0 copy-start.2
  27.9 0.0 copy-start.3
  27.9 0.0 copy-start.4
  27.9 4.6 %pair_bias.1 = (f32[32,48,192]{2,1,0:T(8,128)S(1)}, f32[8,128]{1,0:T(8,128)S(1)}) custom-call(f32[48,192,128]{2,1,0:T(8,128)S(1)} %copy-done, f32[32,128]{1,0:T(8,128)S(1)} %bitcast.15), custom_call_target="tpu_custom_call" | custom-call | flops 452984832 | bytes 5898240 | tf_op jit(solution)/shard_map/pair_bias/pallas_call | solution.py:124
  32.6 0.0 collective-permute-done.2.far_ref
  32.6 3.9 %all-to-all-done.refs_0_ = f32[16,96,128]{2,1,0:T(8,128)S(1)} async-done(((f32[16,96,128]{2,1,0:T(8,128)}), f32[16,96,128]{2,1,0:T(8,128)S(1)}, u32[]{:S(2)}, u32[]{:S(2)}) %all-to-all-start) | async-done | bytes 786464 | tf_op jit(solution)/shard_map/all_to_all | solution.py:365
  36.4 3.1 %collective-permute-start.3 = (f32[16,96,128]{2,1,0:T(8,128)S(1)}, f32[16,96,128]{2,1,0:T(8,128)S(1)}, u32[]{:S(2)}, u32[]{:S(2)}) collective-permute-start(f32[16,96,128]{2,1,0:T(8,128)S(1)} %after.1.own_ref), channel_id=1, source_target_pairs={{0,8},{8,0},{16,24},{24,16},{32,40},{40,32},{48,56},{56,48},{64,72... | collective-permute-start | bytes 2359304 | tf_op jit(solution)/shard_map/ppermute | solution.py:369
  39.5 0.1 pad_add_fusion.place_ref
  39.6 0.0 copy-start.6
  39.6 1.8 %collective-permute-done.3.other_ref = f32[16,96,128]{2,1,0:T(8,128)S(1)} collective-permute-done((f32[16,96,128]{2,1,0:T(8,128)S(1)}, f32[16,96,128]{2,1,0:T(8,128)S(1)}, u32[]{:S(2)}, u32[]{:S(2)}) %collective-permute-start.3) | collective-permute-done | bytes 786464 | tf_op jit(solution)/shard_map/ppermute | solution.py:369
  41.4 2.1 %attention.1 = f32[8,56,128]{2,1,0:T(8,128)S(1)} custom-call(s32[2]{0:T(128)S(1)} %pad_add_fusion.place_ref, f32[4,48,128]{2,1,0:T(8,128)S(1)} %pad_maximum_fusion.q_ref, f32[4,48,128]{2,1,0:T(8,128)S(1)} %collective-permute-done.2.far_ref, f32[16,96,128]{2,1,0:T(8,128)S(1)} %after.1.own_ref, f32[16,96,128]{2,1,0:T(8,128)S(1)} %collective-permute-done.3.other_ref, ...), custom_call_target="tpu_custom_call" | custom-call | tf_op jit(solution)/shard_map/attention/pallas_call | solution.py:199
  43.6 9.9 %all_to_all.20.parts_ref = f32[8,56,128]{2,1,0:T(8,128)S(1)} all-to-all(f32[8,56,128]{2,1,0:T(8,128)S(1)} %attention.1), channel_id=1, replica_groups=mesh['row'=32,'col'=8] {'col'}, dimensions={0} | all-to-all | bytes 458752 | tf_op jit(solution)/shard_map/all_to_all | solution.py:372
  53.4 0.5 merge.1
  53.9 8.5 %all_to_all.21.attn_ref = f32[8,48,128]{2,1,0:T(8,128)S(1)} all-to-all(f32[8,48,128]{2,1,0:T(8,128)S(1)} %merge.1), channel_id=1, replica_groups=mesh['row'=32,'col'=8] {'col'}, dimensions={0} | all-to-all | bytes 393216 | tf_op jit(solution)/shard_map/all_to_all | solution.py:380
  62.4 0.0 copy-done.2
  62.4 0.0 copy-done.3
  62.4 0.0 copy-done.4
  62.4 0.0 copy-done.1
  62.4 0.9 project.1
  63.3 8.4 %all_to_all.22.parts_ref = f32[8,56,128]{2,1,0:T(8,128)S(1)} all-to-all(f32[8,56,128]{2,1,0:T(8,128)S(1)} %get-tuple-element.11), channel_id=1, replica_groups=mesh['row'=32,'col'=8] {'col'}, dimensions={0} | all-to-all | bytes 458752 | tf_op jit(solution)/shard_map/all_to_all | solution.py:390
  71.7 0.3 left_right.1
  72.0 0.0 copy-start.7
  72.0 0.6 copy-done.7
  72.6 1.3 %collective-permute-start.5 = (f32[24,128]{1,0:T(8,128)S(1)}, f32[24,128]{1,0:T(8,128)S(1)}, u32[]{:S(2)}, u32[]{:S(2)}) collective-permute-start(f32[24,128]{1,0:T(8,128)S(1)} %get-tuple-element.13), channel_id=1, source_target_pairs={{0,128},{1,96},{2,160},{3,192},{4,224},{5,0},{6,64},{7,32},{8,136}... | collective-permute-start | bytes 36872 | tf_op jit(solution)/shard_map/ppermute | solution.py:400
  73.9 2.6 %collective-permute-start.4 = (f32[24,128]{1,0:T(8,128)S(1)}, f32[24,128]{1,0:T(8,128)S(1)}, u32[]{:S(2)}, u32[]{:S(2)}) collective-permute-start(f32[24,128]{1,0:T(8,128)S(1)} %get-tuple-element.13), channel_id=1, source_target_pairs={{0,112},{1,144},{2,48},{3,176},{4,16},{5,208},{6,240},{7,80},{8,12... | collective-permute-start | bytes 36872 | tf_op jit(solution)/shard_map/ppermute | solution.py:400
  76.5 1.0 collective-permute-done.5
  77.6 2.8 %collective-permute-done.4 = f32[24,128]{1,0:T(8,128)S(1)} collective-permute-done((f32[24,128]{1,0:T(8,128)S(1)}, f32[24,128]{1,0:T(8,128)S(1)}, u32[]{:S(2)}, u32[]{:S(2)}) %collective-permute-start.4) | collective-permute-done | bytes 12320 | tf_op jit(solution)/shard_map/ppermute | solution.py:400
  80.4 0.0 copy-start.8
  80.4 5.5 %collective-permute-start.6 = (f32[2,24,128]{2,1,0:T(8,128)S(1)}, f32[2,24,128]{2,1,0:T(8,128)S(1)}, u32[]{:S(2)}, u32[]{:S(2)}) collective-permute-start(f32[2,24,128]{2,1,0:T(8,128)S(1)} %pad_maximum_fusion.2.own_ref), channel_id=1, source_target_pairs={{0,8},{8,0},{16,24},{24,16},{32,40},{40,32},{48,56},{56,48},{64,72... | collective-permute-start | bytes 73736 | tf_op jit(solution)/shard_map/ppermute | solution.py:403
  85.8 0.8 collective-permute-done.6.other_ref
  86.7 0.0 copy-start.9
  86.7 0.0 copy-done.6
  86.7 0.0 copy-done.8
  86.7 0.6 copy-done.9
  87.3 22.4 %update_pair.1 = f32[48,192,128]{2,1,0:T(8,128)} custom-call(s32[2]{0:T(128)} %copy-done.6, f32[48,192,128]{2,1,0:T(8,128)} %pair_ref.3, f32[48,128]{1,0:T(8,128)} %copy-done.7, f32[2,24,128]{2,1,0:T(8,128)} %copy-done.8, f32[2,24,128]{2,1,0:T(8,128)} %copy-done.9, f32[128,128]{1,0:T(8,128)} %w_outer_ref.1, f32[1,128]{1,0:T(1,128)} %bitcast.21, ...), custom_call_target="tpu_custom_call" | custom-call | flops 10267656192 | bytes 9437184 | tf_op jit(solution)/shard_map/update_pair/pallas_call | solution.py:287
  (5 shorter events, 0.0 us)
Async XLA Ops:
  2.4 34.1 %all-to-all-start = ((f32[16,96,128]{2,1,0:T(8,128)}), f32[16,96,128]{2,1,0:T(8,128)S(1)}, u32[]{:S(2)}, u32[]{:S(2)}) async-start(f32[16,96,128]{2,1,0:T(8,128)} %pack.1), calls=%async_computation | async-start | bytes 1572864 | tf_op jit(solution)/shard_map/all_to_all | solution.py:365
  14.1 3.2 %collective-permute-start = (f32[1,48,128]{2,1,0:T(8,128)}, f32[1,48,128]{2,1,0:T(8,128)S(1)}, u32[]{:S(2)}, u32[]{:S(2)}) collective-permute-start(f32[1,48,128]{2,1,0:T(8,128)} %bitcast.16), channel_id=1, source_target_pairs={{0,1},{1,0},{2,3},{3,2},{4,5},{5,4},{6,7},{7,6},{8,9},{9,8},{10,11... | collective-permute-start | bytes 73736 | tf_op jit(solution)/shard_map/ppermute | solution.py:362
  18.1 3.2 %collective-permute-start.1 = (f32[2,48,128]{2,1,0:T(8,128)S(1)}, f32[2,48,128]{2,1,0:T(8,128)S(1)}, u32[]{:S(2)}, u32[]{:S(2)}) collective-permute-start(f32[2,48,128]{2,1,0:T(8,128)S(1)} %pad_maximum_fusion.1), channel_id=1, source_target_pairs={{0,2},{1,3},{2,0},{3,1},{4,6},{5,7},{6,4},{7,5},{8,10},{9,11},{10,... | collective-permute-start | bytes 147464 | tf_op jit(solution)/shard_map/ppermute | solution.py:362
  22.1 10.5 %collective-permute-start.2 = (f32[4,48,128]{2,1,0:T(8,128)S(1)}, f32[4,48,128]{2,1,0:T(8,128)S(1)}, u32[]{:S(2)}, u32[]{:S(2)}) collective-permute-start(f32[4,48,128]{2,1,0:T(8,128)S(1)} %pad_maximum_fusion.q_ref), channel_id=1, source_target_pairs={{0,4},{1,5},{2,6},{3,7},{4,0},{5,1},{6,2},{7,3},{8,12},{9,13},{10,... | collective-permute-start | bytes 294920 | tf_op jit(solution)/shard_map/ppermute | solution.py:362
  24.8 2.3 %copy-start = (f32[48,192,128]{2,1,0:T(8,128)S(1)}, f32[48,192,128]{2,1,0:T(8,128)}, u32[]{:S(2)}) copy-start(f32[48,192,128]{2,1,0:T(8,128)} %pair_ref.3) | copy-start | bytes 14155780
  27.2 0.7 copy-start.5
  27.9 34.5 %copy-start.2 = (f32[128,64]{0,1:T(8,128)S(1)}, f32[128,64]{0,1:T(8,128)}, u32[]{:S(2)}) copy-start(f32[128,64]{0,1:T(8,128)} %param.20) | copy-start | bytes 98308
  27.9 34.5 %copy-start.3 = (f32[128,64]{0,1:T(8,128)S(1)}, f32[128,64]{0,1:T(8,128)}, u32[]{:S(2)}) copy-start(f32[128,64]{0,1:T(8,128)} %param.21) | copy-start | bytes 98308
  27.9 34.5 %copy-start.4 = (f32[48,128]{1,0:T(8,128)S(1)}, f32[48,128]{1,0:T(8,128)}, u32[]{:S(2)}) copy-start(f32[48,128]{1,0:T(8,128)} %seq_ref.1) | copy-start | bytes 73732
  36.4 5.0 %collective-permute-start.3 = (f32[16,96,128]{2,1,0:T(8,128)S(1)}, f32[16,96,128]{2,1,0:T(8,128)S(1)}, u32[]{:S(2)}, u32[]{:S(2)}) collective-permute-start(f32[16,96,128]{2,1,0:T(8,128)S(1)} %after.1.own_ref), channel_id=1, source_target_pairs={{0,8},{8,0},{16,24},{24,16},{32,40},{40,32},{48,56},{56,48},{64,72... | collective-permute-start | bytes 2359304 | tf_op jit(solution)/shard_map/ppermute | solution.py:369
  39.5 22.9 %copy-start.1 = (f32[1024,128]{1,0:T(8,128)S(1)}, f32[1024,128]{1,0:T(8,128)}, u32[]{:S(2)}) copy-start(f32[1024,128]{1,0:T(8,128)} %w_out_ref.1) | copy-start | bytes 1572868
  39.6 47.1 %copy-start.6 = (s32[2]{0:T(128)}, s32[2]{0:T(128)S(1)}, u32[]{:S(2)}) copy-start(s32[2]{0:T(128)S(1)} %pad_add_fusion.place_ref) | copy-start | bytes 28
  72.0 0.6 copy-start.7
  72.6 4.9 %collective-permute-start.5 = (f32[24,128]{1,0:T(8,128)S(1)}, f32[24,128]{1,0:T(8,128)S(1)}, u32[]{:S(2)}, u32[]{:S(2)}) collective-permute-start(f32[24,128]{1,0:T(8,128)S(1)} %get-tuple-element.13), channel_id=1, source_target_pairs={{0,128},{1,96},{2,160},{3,192},{4,224},{5,0},{6,64},{7,32},{8,136}... | collective-permute-start | bytes 36872 | tf_op jit(solution)/shard_map/ppermute | solution.py:400
  73.9 6.5 %collective-permute-start.4 = (f32[24,128]{1,0:T(8,128)S(1)}, f32[24,128]{1,0:T(8,128)S(1)}, u32[]{:S(2)}, u32[]{:S(2)}) collective-permute-start(f32[24,128]{1,0:T(8,128)S(1)} %get-tuple-element.13), channel_id=1, source_target_pairs={{0,112},{1,144},{2,48},{3,176},{4,16},{5,208},{6,240},{7,80},{8,12... | collective-permute-start | bytes 36872 | tf_op jit(solution)/shard_map/ppermute | solution.py:400
  80.4 6.3 %copy-start.8 = (f32[2,24,128]{2,1,0:T(8,128)}, f32[2,24,128]{2,1,0:T(8,128)S(1)}, u32[]{:S(2)}) copy-start(f32[2,24,128]{2,1,0:T(8,128)S(1)} %pad_maximum_fusion.2.own_ref) | copy-start | bytes 73732
  80.4 6.3 %collective-permute-start.6 = (f32[2,24,128]{2,1,0:T(8,128)S(1)}, f32[2,24,128]{2,1,0:T(8,128)S(1)}, u32[]{:S(2)}, u32[]{:S(2)}) collective-permute-start(f32[2,24,128]{2,1,0:T(8,128)S(1)} %pad_maximum_fusion.2.own_ref), channel_id=1, source_target_pairs={{0,8},{8,0},{16,24},{24,16},{32,40},{40,32},{48,56},{56,48},{64,72... | collective-permute-start | bytes 73736 | tf_op jit(solution)/shard_map/ppermute | solution.py:403
  86.7 0.6 copy-start.9
